TPU v7x, 512 devices: a whole 4x8x8 slice. The times are simulated.
512 devices in a mesh: lat: 16 (over x, y_hi), lon: 32 (over y_lo, z, core).
Axes of the slice: x: 4, y: 8 (y_hi: 4, y_lo: 2; y = y_hi * 2 + y_lo), z: 8, core: 2. Of those that a mesh axis runs over, the one named last changes fastest.
Arguments:
- level_tokens: bfloat16 [13, 96, 384, 512], P(None, 'lat', 'lon'), may hold values from -6 to 6
- hidden_probe_match_matrix: bfloat16 [3, 16, 512], replicated, may hold values from -0.5 to 0.5
- value_weight: bfloat16 [512, 512], P('lon'), may hold values from -0.25 to 0.25
- pool_out_weight: bfloat16 [512, 512], P('lon'), may hold values from -0.25 to 0.25
- latent_base: bfloat16 [3, 512], replicated, may hold values from -5 to 5
- norm_gain: float32 [512], replicated, may hold values from 0.25 to 1.75
- qkv_weight: bfloat16 [512, 1536], P('lon'), may hold values from -0.25 to 0.25
- attn_out_weight: bfloat16 [512, 512], P('lon'), may hold values from -0.25 to 0.25
- region_ids: int32 [96, 384], P('lat', 'lon'), may hold values from 0 to 3, as said below
Outputs:
- latent_out: bfloat16 [3, 96, 384, 512], P(None, 'lat', 'lon')
Inputs may be any that keep to these rules, and one draw needn't show every extreme that they name: region_ids is constant on each block of 3 rows by 6 columns aligned to multiples of these sizes.
All inputs are finite; a program needn't handle non-finite values.
Results may differ from a plain program's by a relative error of at most 0.019.
Values may be sent and summed in bfloat16 or wider, within the bound.
No kernel may reach another device: no remote copies, remote signals or barrier semaphores. Data moves between devices by JAX's collectives and lax.ppermute only.
A program may use at most 64 MiB of HBM per device.

v0:
```python
import jax
import jax.numpy as jnp
from jax import lax
from jax.sharding import PartitionSpec as P

HEADS = 8
LATENTS = 3
WIN_LAT = 6
WIN_LON = 12


STABILIZER_TINY = 1e-05


def shifted_2(block, axis, distance):
    devices = range(lax.axis_size(axis))
    route = [((i - distance) % len(devices), i) for i in devices]
    return lax.ppermute(block, axis, route)


def layer_norm(latent, norm_gain):
    padded_zonal_band = latent.astype(jnp.float32)
    mean_val = jnp.mean(padded_zonal_band, axis=-1, keepdims=True)
    centred = padded_zonal_band - mean_val
    variance = jnp.mean(centred * centred, axis=-1, keepdims=True)
    return (centred * lax.rsqrt(variance + STABILIZER_TINY) * norm_gain).astype(jnp.bfloat16)


def attend(projected, levels, row_count, col_count, labels, head_count):
    model_width = projected.shape[-1] // 3
    head_dim = model_width // head_count
    lat_win = row_count // WIN_LAT
    lon_win = col_count // WIN_LON
    window_len = levels * WIN_LAT * WIN_LON
    split_up = projected.reshape(
        levels, lat_win, WIN_LAT, lon_win, WIN_LON, 3, head_count, head_dim
    )
    split_up = jnp.transpose(split_up, (5, 1, 3, 6, 0, 2, 4, 7))
    split_up = split_up.reshape(3, lat_win * lon_win, head_count, window_len, head_dim)
    summary_logits = (
        jnp.einsum("whad,whbd->whab", split_up[0], split_up[1], preferred_element_type=jnp.float32)
        / head_dim**0.5
    )
    grouped = labels.reshape(lat_win, WIN_LAT, lon_win, WIN_LON).transpose(0, 2, 1, 3)
    grouped = grouped.reshape(lat_win * lon_win, 1, WIN_LAT * WIN_LON)
    grouped = jnp.broadcast_to(grouped, (lat_win * lon_win, levels, WIN_LAT * WIN_LON))
    grouped = grouped.reshape(lat_win * lon_win, window_len)
    allowed = grouped[:, :, None] == grouped[:, None, :]
    summary_logits = jnp.where(allowed[:, None], summary_logits, -1e30)
    weights = jax.nn.softmax(summary_logits, axis=-1).astype(jnp.bfloat16)
    attended = jnp.einsum(
        "whab,whbd->whad", weights, split_up[2], preferred_element_type=jnp.float32
    ).astype(jnp.bfloat16)
    attended = attended.reshape(lat_win, lon_win, head_count, levels, WIN_LAT, WIN_LON, head_dim)
    attended = jnp.transpose(attended, (3, 0, 4, 1, 5, 2, 6))
    return attended.reshape(levels * row_count * col_count, model_width)


def row_product(left_rows, weight_piece):
    return jnp.dot(left_rows, weight_piece, preferred_element_type=jnp.float32)


def body(
    level_tokens,
    hidden_probe_match_matrix,
    value_weight,
    pool_out_weight,
    latent_base,
    norm_gain,
    qkv_weight,
    attn_out_weight,
    region_ids,
):
    levels, row_count, col_count, model_width = level_tokens.shape
    pool_count = hidden_probe_match_matrix.shape[1]
    summary_width = model_width // pool_count
    positions = row_count * col_count
    isobar_token_matrix = level_tokens.reshape(levels, positions, model_width)
    summary_logits = jnp.einsum(
        "lep,qdp->qdel",
        isobar_token_matrix,
        hidden_probe_match_matrix,
        preferred_element_type=jnp.float32,
    )
    weights = jax.nn.softmax(summary_logits, axis=-1).astype(jnp.bfloat16)

    def pool_one(latent_weights):
        return jnp.einsum(
            "hpl,lpd->hpd", latent_weights, isobar_token_matrix, preferred_element_type=jnp.float32
        ).astype(jnp.bfloat16)

    pooled = lax.map(pool_one, weights)
    weight_piece = lax.all_gather(value_weight, "lon", axis=0, tiled=True)
    count_rows = weight_piece.shape[0]
    per_head = weight_piece.reshape(count_rows, pool_count, summary_width)
    pool_values = jnp.einsum("mhpd,dhe->mphe", pooled, per_head, preferred_element_type=jnp.float32)
    pool_values = pool_values.reshape(LATENTS * positions, model_width).astype(jnp.bfloat16)
    mixed_sum = row_product(pool_values, lax.all_gather(pool_out_weight, "lon", axis=0, tiled=True))
    mixed_sum = mixed_sum.reshape(LATENTS, positions, model_width)
    latent = (latent_base.astype(jnp.float32)[:, None, :] + mixed_sum).astype(jnp.bfloat16)
    latent = latent.reshape(LATENTS, row_count, col_count, model_width)
    normed = layer_norm(latent, norm_gain)
    half_lat = WIN_LAT // 2
    half_longitude = WIN_LON // 2
    from_east = shifted_2(normed[:, :, :half_longitude], "lon", -1)
    east_joined = jnp.concatenate([normed[:, :, half_longitude:], from_east], axis=2)
    from_south = shifted_2(east_joined[:, :half_lat], "lat", -1)
    shifted = jnp.concatenate([east_joined[:, half_lat:], from_south], axis=1)
    meridian_patch_total = row_count * lax.axis_size("lat")
    global_rows = lax.axis_index("lat") * row_count + jnp.arange(row_count, dtype=jnp.int32)
    wrapped_longitude = (global_rows >= meridian_patch_total - half_lat).astype(jnp.int32)
    labels = region_ids * 2 + wrapped_longitude[:, None]
    token_rows = shifted.reshape(LATENTS * positions, model_width)
    qkv_whole, attn_out_whole = (
        lax.all_gather(qkv_weight, "lon", axis=0, tiled=True),
        lax.all_gather(attn_out_weight, "lon", axis=0, tiled=True),
    )
    projected = jnp.dot(token_rows, qkv_whole, preferred_element_type=jnp.float32).astype(
        jnp.bfloat16
    )
    attended = attend(projected, LATENTS, row_count, col_count, labels, HEADS)
    attn_proj = jnp.dot(attended, attn_out_whole, preferred_element_type=jnp.float32)
    attn_proj = attn_proj.astype(jnp.bfloat16).reshape(LATENTS, row_count, col_count, model_width)
    from_north = shifted_2(attn_proj[:, row_count - half_lat :], "lat", 1)
    northern_joined = jnp.concatenate([from_north, attn_proj[:, : row_count - half_lat]], axis=1)
    from_west = shifted_2(northern_joined[:, :, col_count - half_longitude :], "lon", 1)
    restored = jnp.concatenate(
        [from_west, northern_joined[:, :, : col_count - half_longitude]], axis=2
    )
    return (latent.astype(jnp.float32) + restored.astype(jnp.float32)).astype(jnp.bfloat16)


def solution(mesh):
    placed = (
        P(None, "lat", "lon", None),
        P(),
        P("lon", None),
        P("lon", None),
        P(),
        P(),
        P("lon", None),
        P("lon", None),
        P("lat", "lon"),
    )
    return jax.shard_map(
        body, mesh=mesh, in_specs=placed, out_specs=P(None, "lat", "lon", None), check_vma=False
    )
```

profile of v0, /device:TPU:1, one launch (start us, length us, event | category | flops | bytes accessed | tf_op | source)
XLA Modules:
  0.0 182.9 jit_solution(6571015992232813151)
XLA Ops:
  6.5 0.7 all-gather.2.cloned.1.call-update
  7.3 0.1 copy-done
  7.3 2.5 %fusion.39 = (f32[3,16,72]{2,1,0:T(8,128)S(1)}, f32[3,16,72,13]{2,1,3,0:T(8,128)S(1)}) fusion(bf16[13,72,512]{2,0,1:T(8,128)(2,1)} %bitcast.62, bf16[3,16,512]{2,1,0:T(8,128)(2,1)S(1)} %copy-done), kind=kOutput, calls=%fused_computation.57 | convolution fusion | flops 46047744 | bytes 1201152 | tf_op jit(solution)/shard_map/lep,qdp->qdel/dot_general | solution.py:79
  9.8 0.1 fusion.18
  9.9 0.1 divide_convert_fusion.2
  10.0 7.4 %while.10 = (s32[]{:T(128)}, bf16[3,16,72,512]{3,2,0,1:T(8,128)(2,1)}, bf16[3,16,72,13]{2,1,3,0:T(8,128)(2,1)S(1)}, bf16[13,72,512]{2,0,1:T(8,128)(2,1)S(1)}, s32[]{:T(128)}) while((s32[]{:T(128)}, bf16[3,16,72,512]{3,2,0,1:T(8,128)(2,1)}, bf16[3,16,72,13]{2,1,3,0:T(8,128)(2,1)S(1)}, bf16[13,72,512]{2,0,1:T(8,128)(2,1)S(1)}, s32[]{:T(128)}) %tuple.33), condition=%wide.region_3.4_spmd, body=%wide.region_2.3_spmd.sunk | while | flops 15925250 | bytes 4647745 | solution.py:92
  10.0 0.3 copy.71
  10.3 0.4 fusion.59
  10.8 1.7 copy_dynamic-update-slice_fusion.2
  12.5 0.3 copy.71
  12.8 0.5 fusion.59
  13.2 1.7 copy_dynamic-update-slice_fusion.2
  14.9 0.3 copy.71
  15.2 0.4 fusion.59
  15.7 1.7 copy_dynamic-update-slice_fusion.2
  17.4 43.3 %all_gather.12 = bf16[512,512]{1,0:T(8,128)(2,1)S(1)} all-gather(bf16[16,512]{1,0:T(8,128)(2,1)S(1)} %copy-done.2), channel_id=1, replica_groups=mesh['lat'=16,'lon'=32] {'lon'}, dimensions={0}, use_global_device_ids=true | all-gather | bytes 540672 | tf_op jit(solution)/shard_map/all_gather | solution.py:93
  60.7 0.2 copy.20
  60.9 3.3 %fusion.4 = bf16[3,72,16,32]{1,3,0,2:T(8,128)(2,1)S(1)} fusion(bf16[3,16,72,512]{3,2,0,1:T(8,128)(2,1)} %get-tuple-element.27, bf16[512,16,32,1]{0,2,3,1:T(8,128)(2,1)S(1)} %bitcast.65), kind=kOutput, calls=%fused_computation.14 | convolution fusion | flops 113356800 | bytes 4284416 | tf_op jit(solution)/shard_map/mhpd,dhe->mphe/dot_general | solution.py:96
  64.3 32.2 %all_gather.13 = bf16[512,512]{1,0:T(8,128)(2,1)S(1)} all-gather(bf16[16,512]{1,0:T(8,128)(2,1)S(1)} %copy-done.3), channel_id=1, replica_groups=mesh['lat'=16,'lon'=32] {'lon'}, dimensions={0}, use_global_device_ids=true | all-gather | bytes 540672 | tf_op jit(solution)/shard_map/all_gather | solution.py:98
  96.5 0.4 fusion.40
  97.0 0.1 div.34
  97.1 0.2 multiply_reduce_fusion
  97.3 0.1 rsqrt.12
  97.4 0.2 multiply_convert_fusion
  97.6 2.1 %collective-permute-start = (bf16[3,6,6,512]{3,2,1,0:T(8,128)(2,1)S(1)}, bf16[3,6,6,512]{3,2,1,0:T(8,128)(2,1)S(1)}, u32[]{:S(2)}, u32[]{:S(2)}) collective-permute-start(bf16[3,6,6,512]{3,2,1,0:T(8,128)(2,1)S(1)} %get-tuple-element.52), channel_id=1, source_target_pairs={{1,0},{2,1},{3,2},{4,3},{5,4},{6,5},{7,6},{8,7},{9,8},{10,9},{11,1... | collective-permute-start | bytes 331784 | tf_op jit(solution)/shard_map/ppermute | solution.py:18
  99.7 34.2 %all_gather.15 = bf16[512,512]{1,0:T(8,128)(2,1)S(1)} all-gather(bf16[16,512]{1,0:T(8,128)(2,1)S(1)} %copy-done.4), channel_id=1, replica_groups=mesh['lat'=16,'lon'=32] {'lon'}, dimensions={0}, use_global_device_ids=true | all-gather | bytes 540672 | tf_op jit(solution)/shard_map/all_gather | solution.py:116
  133.9 0.1 multiply_add_fusion
  134.0 0.1 broadcast_in_dim.23
  134.1 0.1 eq.21
  134.2 0.1 fusion.20
  134.3 7.4 %collective-permute-start.1 = (bf16[3,3,12,512]{3,2,1,0:T(8,128)(2,1)S(1)}, bf16[3,3,12,512]{3,2,1,0:T(8,128)(2,1)S(1)}, u32[]{:S(2)}, u32[]{:S(2)}) collective-permute-start(bf16[3,3,12,512]{3,2,1,0:T(8,128)(2,1)S(1)} %get-tuple-element.50), channel_id=1, source_target_pairs={{32,0},{64,32},{96,64},{128,96},{160,128},{192,160},{224,192},{256... | collective-permute-start | bytes 331784 | tf_op jit(solution)/shard_map/ppermute | solution.py:18
  141.7 0.1 broadcast_compare_fusion
  141.8 4.3 %collective-permute-done.1 = bf16[3,3,12,512]{3,2,1,0:T(8,128)(2,1)S(1)} collective-permute-done((bf16[3,3,12,512]{3,2,1,0:T(8,128)(2,1)S(1)}, bf16[3,3,12,512]{3,2,1,0:T(8,128)(2,1)S(1)}, u32[]{:S(2)}, u32[]{:S(2)}) %collective-permute-start.1) | collective-permute-done | bytes 110624 | tf_op jit(solution)/shard_map/ppermute | solution.py:18
  146.3 1.9 %convolution_convert_fusion.1 = bf16[216,1536]{1,0:T(8,128)(2,1)S(1)} fusion(bf16[216,512]{1,0:T(8,128)(2,1)S(1)} %reshape.161, bf16[512,1536]{1,0:T(8,128)(2,1)} %all-gather.2.cloned.1.call-done), kind=kOutput, calls=%fused_computation.6 | convolution fusion | flops 340070400 | bytes 2457600 | tf_op jit(solution)/shard_map/dot_general | solution.py:118
  148.2 0.7 reshape.162
  149.0 0.3 copy.67
  149.2 0.1 fusion.36
  149.3 2.0 %fusion.41 = (f32[8,216]{1,0:T(8,128)S(1)}, f32[8,216,216]{1,2,0:T(8,128)}) fusion(pred[216,216]{0,1:T(8,128)(4,1)S(1)} %broadcast_compare_fusion, bf16[8,216,64]{2,0,1:T(8,128)(2,1)S(1)} %bitcast.69, bf16[8,216,64]{2,0,1:T(8,128)(2,1)S(1)} %bitcast.70), kind=kOutput, calls=%fused_computation.59 | convolution fusion | flops 49268952 | bytes 1988928 | tf_op jit(solution)/shard_map/sub | solution.py:50
  151.3 1.8 convolution_convert_fusion.3
  153.1 0.3 copy.29
  153.4 0.3 reshape.167
  153.7 0.3 convolution_convert_fusion.4
  154.0 5.4 %collective-permute-start.2 = (bf16[3,3,12,512]{3,2,1,0:T(8,128)(2,1)S(1)}, bf16[3,3,12,512]{3,2,1,0:T(8,128)(2,1)S(1)}, u32[]{:S(2)}, u32[]{:S(2)}) collective-permute-start(bf16[3,3,12,512]{3,2,1,0:T(8,128)(2,1)S(1)} %get-tuple-element.47), channel_id=1, source_target_pairs={{480,0},{0,32},{32,64},{64,96},{96,128},{128,160},{160,192},{192,2... | collective-permute-start | bytes 331784 | tf_op jit(solution)/shard_map/ppermute | solution.py:18
  159.4 4.7 %collective-permute-done.2 = bf16[3,3,12,512]{3,2,1,0:T(8,128)(2,1)S(1)} collective-permute-done((bf16[3,3,12,512]{3,2,1,0:T(8,128)(2,1)S(1)}, bf16[3,3,12,512]{3,2,1,0:T(8,128)(2,1)S(1)}, u32[]{:S(2)}, u32[]{:S(2)}) %collective-permute-start.2) | collective-permute-done | bytes 110624 | tf_op jit(solution)/shard_map/ppermute | solution.py:18
  164.1 0.1 fusion.19
  164.2 8.9 %collective-permute-start.3 = (bf16[3,6,6,512]{3,2,1,0:T(8,128)(2,1)S(1)}, bf16[3,6,6,512]{3,2,1,0:T(8,128)(2,1)S(1)}, u32[]{:S(2)}, u32[]{:S(2)}) collective-permute-start(bf16[3,6,6,512]{3,2,1,0:T(8,128)(2,1)S(1)} %fusion.19), channel_id=1, source_target_pairs={{31,0},{0,1},{1,2},{2,3},{3,4},{4,5},{5,6},{6,7},{7,8},{8,9},{9,10... | collective-permute-start | bytes 331784 | tf_op jit(solution)/shard_map/ppermute | solution.py:18
  173.2 2.1 %collective-permute-done.3 = bf16[3,6,6,512]{3,2,1,0:T(8,128)(2,1)S(1)} collective-permute-done((bf16[3,6,6,512]{3,2,1,0:T(8,128)(2,1)S(1)}, bf16[3,6,6,512]{3,2,1,0:T(8,128)(2,1)S(1)}, u32[]{:S(2)}, u32[]{:S(2)}) %collective-permute-start.3) | collective-permute-done | bytes 110624 | tf_op jit(solution)/shard_map/ppermute | solution.py:18
  175.2 0.9 add_convert_fusion
  (34 shorter events, 0.4 us)
Async XLA Ops:
  6.5 0.8 copy-start
  6.5 3.4 %copy-start.1 = (bf16[13,6,12,512]{3,0,2,1:T(8,128)(2,1)S(1)}, bf16[13,6,12,512]{3,0,2,1:T(8,128)(2,1)}, u32[]{:S(2)}) copy-start(bf16[13,6,12,512]{3,0,2,1:T(8,128)(2,1)} %param.11) | copy-start | bytes 2875396
  6.5 139.7 %all-gather.2.cloned.1.call-start = ((), (), s32[]{:S(2)}) async-start(), calls=%async_computation | async-start | bytes 1622016 | tf_op jit(solution)/shard_map/all_gather | solution.py:115
  9.9 7.4 %copy-start.2 = (bf16[16,512]{1,0:T(8,128)(2,1)S(1)}, bf16[16,512]{1,0:T(8,128)(2,1)}, u32[]{:S(2)}) copy-start(bf16[16,512]{1,0:T(8,128)(2,1)} %param.13) | copy-start | bytes 49156
  60.9 3.4 %copy-start.5 = (bf16[3,512]{1,0:T(4,128)(2,1)S(1)}, bf16[3,512]{1,0:T(4,128)(2,1)}, u32[]{:S(2)}) copy-start(bf16[3,512]{1,0:T(4,128)(2,1)} %param.15) | copy-start | bytes 9220
  60.9 3.4 %copy-start.3 = (bf16[16,512]{1,0:T(8,128)(2,1)S(1)}, bf16[16,512]{1,0:T(8,128)(2,1)}, u32[]{:S(2)}) copy-start(bf16[16,512]{1,0:T(8,128)(2,1)} %param.14) | copy-start | bytes 49156
  64.2 33.1 %copy-start.7 = (f32[512]{0:T(512)S(1)}, f32[512]{0:T(512)}, u32[]{:S(2)}) copy-start(f32[512]{0:T(512)} %param.16) | copy-start | bytes 6148
  96.9 2.8 %copy-start.4 = (bf16[16,512]{1,0:T(8,128)(2,1)S(1)}, bf16[16,512]{1,0:T(8,128)(2,1)}, u32[]{:S(2)}) copy-start(bf16[16,512]{1,0:T(8,128)(2,1)} %param.18) | copy-start | bytes 49156
  96.9 37.0 %copy-start.6 = (s32[6,12]{1,0:T(8,128)S(1)}, s32[6,12]{1,0:T(8,128)}, u32[]{:S(2)}) copy-start(s32[6,12]{1,0:T(8,128)} %param.19) | copy-start | bytes 868
  97.6 36.5 %collective-permute-start = (bf16[3,6,6,512]{3,2,1,0:T(8,128)(2,1)S(1)}, bf16[3,6,6,512]{3,2,1,0:T(8,128)(2,1)S(1)}, u32[]{:S(2)}, u32[]{:S(2)}) collective-permute-start(bf16[3,6,6,512]{3,2,1,0:T(8,128)(2,1)S(1)} %get-tuple-element.52), channel_id=1, source_target_pairs={{1,0},{2,1},{3,2},{4,3},{5,4},{6,5},{7,6},{8,7},{9,8},{10,9},{11,1... | collective-permute-start | bytes 331784 | tf_op jit(solution)/shard_map/ppermute | solution.py:18
  134.3 11.9 %collective-permute-start.1 = (bf16[3,3,12,512]{3,2,1,0:T(8,128)(2,1)S(1)}, bf16[3,3,12,512]{3,2,1,0:T(8,128)(2,1)S(1)}, u32[]{:S(2)}, u32[]{:S(2)}) collective-permute-start(bf16[3,3,12,512]{3,2,1,0:T(8,128)(2,1)S(1)} %get-tuple-element.50), channel_id=1, source_target_pairs={{32,0},{64,32},{96,64},{128,96},{160,128},{192,160},{224,192},{256... | collective-permute-start | bytes 331784 | tf_op jit(solution)/shard_map/ppermute | solution.py:18
  154.0 10.1 %collective-permute-start.2 = (bf16[3,3,12,512]{3,2,1,0:T(8,128)(2,1)S(1)}, bf16[3,3,12,512]{3,2,1,0:T(8,128)(2,1)S(1)}, u32[]{:S(2)}, u32[]{:S(2)}) collective-permute-start(bf16[3,3,12,512]{3,2,1,0:T(8,128)(2,1)S(1)} %get-tuple-element.47), channel_id=1, source_target_pairs={{480,0},{0,32},{32,64},{64,96},{96,128},{128,160},{160,192},{192,2... | collective-permute-start | bytes 331784 | tf_op jit(solution)/shard_map/ppermute | solution.py:18
  164.2 11.0 %collective-permute-start.3 = (bf16[3,6,6,512]{3,2,1,0:T(8,128)(2,1)S(1)}, bf16[3,6,6,512]{3,2,1,0:T(8,128)(2,1)S(1)}, u32[]{:S(2)}, u32[]{:S(2)}) collective-permute-start(bf16[3,6,6,512]{3,2,1,0:T(8,128)(2,1)S(1)} %fusion.19), channel_id=1, source_target_pairs={{31,0},{0,1},{1,2},{2,3},{3,4},{4,5},{5,6},{6,7},{7,8},{8,9},{9,10... | collective-permute-start | bytes 331784 | tf_op jit(solution)/shard_map/ppermute | solution.py:18
Sparse Core Ops, SparseCore 0:
  9.5 73.4 all-gather.1
where the time goes:
time: 184 us; the launch traced here: 183 us
  blocking collectives  110 us (60%)
  starting transfers between devices  23.8 us (13%)
  between operations  13.7 us (7%)
  matrix products  13.4 us (7%)
  waiting for transfers between devices  11.8 us (6%)
  local copies, waits for them, and re-layouts  8.57 us (5%)
    all_gather x1, blocking collectives, body(): weight_piece = lax.all_gather(value_weight, 'lon', axis=0, tiled=True)  43.3 us
    all_gather x1, blocking collectives, body(): lax.all_gather(attn_out_weight, 'lon', axis=0, tiled=True)  34.2 us
    all_gather x1, blocking collectives, body(): lax.all_gather(pool_out_weight, 'lon', axis=0, tiled=True)  32.2 us
    ppermute x4, starting transfers between devices, shifted_2(): return lax.ppermute(block, axis, route)  23.8 us
    ppermute x4, waiting for transfers between devices, shifted_2(): return lax.ppermute(block, axis, route)  11.1 us
    dynamic_update_slice x3, local copies, waits for them, and re-layouts, body(): pooled = lax.map(pool_one, weights)  5.05 us
  transfers between devices with their start and end apart: 5, of which 3 were waited for; matrix products, arithmetic and copies ran while one was open for 8% of the time, Pallas kernels for 0%

commit v1 on v0

v1 whole, which is shorter than its diff:
```python
import functools

import jax
import jax.numpy as jnp
from jax import lax
from jax.experimental import pallas as pl
from jax.experimental.pallas import tpu as pltpu
from jax.sharding import PartitionSpec as P

HEADS = 8
LATENTS = 3
WIN_LAT = 6
WIN_LON = 12
HALF_LAT = WIN_LAT // 2
HALF_LON = WIN_LON // 2
CELLS = HALF_LAT * HALF_LON
PADDED = 80
LAT_RING = 4
STABILIZER_TINY = 1e-05
BOTH = ("lat", "lon")


def pairs(source_of, lat_count, lon_count):
    route = []
    for i in range(lat_count):
        for j in range(lon_count):
            si, sj = source_of(i, j)
            source = (si % lat_count) * lon_count + sj % lon_count
            route.append((source, i * lon_count + j))
    return route


def fetch(block, source_of):
    route = pairs(source_of, lax.axis_size("lat"), lax.axis_size("lon"))
    return lax.ppermute(block, BOTH, route)


def give_back(block, source_of):
    route = pairs(source_of, lax.axis_size("lat"), lax.axis_size("lon"))
    return lax.ppermute(block, BOTH, [(b, a) for a, b in route])


def band_of(j):
    return 1 if j % 2 == 0 else -1


def beside(i, j):
    return i, j + 1


def along(i, j):
    return i + band_of(j), j


def across(i, j):
    return i + band_of(j), j + 1


def slice_step(dx, dy):
    def source_of(i, j):
        x, y = i // LAT_RING, i % LAT_RING
        step = dy * band_of(j)
        return ((x + dx) % LAT_RING) * LAT_RING + (y + step) % LAT_RING, j

    return source_of


SLICE_STEPS = ((2, slice_step(0, 1)), (1, slice_step(1, 0)), (3, slice_step(-1, 0)))


def other_core(i, j):
    return i, j + 1 if j % 2 == 0 else j - 1


def window_kernel(
    heads,
    pool_heads,
    place,
    tokens,
    probe,
    own_slices,
    other_slices,
    base,
    gain,
    out,
    weights,
    values,
):
    level_count, cells, width = tokens.shape
    latents = base.shape[0]
    shares = own_slices.shape[0]
    columns = own_slices.shape[2]
    f32 = jnp.float32
    bf16 = jnp.bfloat16
    quad, core = place[0], place[1]
    shifts = (0,) + tuple(step for step, _ in SLICE_STEPS)
    for ref, side in ((own_slices, core), (other_slices, 1 - core)):
        for s in range(shares):
            start = (lax.rem(quad + shifts[s], shares) * 2 + side) * columns
            weights[:, pl.ds(pl.multiple_of(start, 128), columns)] = ref[s]

    x = tokens[...].reshape(level_count * cells, width)
    scores = lax.dot_general(x, probe[...], (((1,), (1,)), ((), ())), preferred_element_type=f32)
    scores = scores.reshape(level_count, cells, latents * pool_heads)
    scores = jnp.exp(scores - jnp.max(scores, axis=0, keepdims=True))
    mix = scores / jnp.sum(scores, axis=0, keepdims=True)
    mix = mix.astype(bf16).reshape(level_count * cells, latents * pool_heads)
    values[...] = jnp.dot(x, weights[:, :width], preferred_element_type=f32)
    span = width // pool_heads
    head_of = lax.broadcasted_iota(jnp.int32, (latents * pool_heads, width), 1) // span
    row_of = lax.broadcasted_iota(jnp.int32, (latents * pool_heads, width), 0)
    pooled = []
    for m in range(latents):
        spread = jnp.where(row_of == head_of + m * pool_heads, 1.0, 0.0).astype(bf16)
        share = jnp.dot(mix, spread, preferred_element_type=f32) * values[...]
        pooled.append(jnp.sum(share.reshape(level_count, cells, width), axis=0).astype(bf16))
    pooled = jnp.concatenate(pooled, axis=0)
    latent = jnp.dot(pooled, weights[:, width : 2 * width], preferred_element_type=f32)
    base_rows = jnp.broadcast_to(base[...].astype(f32)[:, None, :], (latents, cells, width))
    latent = (latent + base_rows.reshape(latents * cells, width)).astype(bf16)

    full = latent.astype(f32)
    centred = full - jnp.mean(full, axis=-1, keepdims=True)
    variance = jnp.mean(centred * centred, axis=-1, keepdims=True)
    normed = (centred * lax.rsqrt(variance + STABILIZER_TINY) * gain[...]).astype(bf16)
    qkv = jnp.dot(normed, weights[:, 2 * width : 5 * width], preferred_element_type=f32)
    qkv = qkv.astype(bf16)

    tokens_in = latents * cells
    quarter_labels = [place[2 + k] for k in range(4)]

    def labels_of(shape, axis):
        cell = lax.rem(lax.broadcasted_iota(jnp.int32, shape, axis), cells)
        label = jnp.full(shape, -1, jnp.int32)
        for k in range(3, -1, -1):
            label = jnp.where(cell < CELLS * (k + 1), quarter_labels[k], label)
        return label

    allowed = labels_of((tokens_in, tokens_in), 0) == labels_of((tokens_in, tokens_in), 1)
    head_dim = width // heads
    pair = 2 * head_dim
    lane = lax.broadcasted_iota(jnp.int32, (1, pair), 1)
    left = jnp.where(lane < head_dim, 1.0, 0.0)
    sides = (left.astype(bf16), (1.0 - left).astype(bf16))
    attended = []
    for h in range(heads // 2):
        q = qkv[:, h * pair : (h + 1) * pair]
        k = qkv[:, width + h * pair : width + (h + 1) * pair]
        v = qkv[:, 2 * width + h * pair : 2 * width + (h + 1) * pair]
        both = []
        for side in sides:
            logits = lax.dot_general(
                q * side, k, (((1,), (1,)), ((), ())), preferred_element_type=f32
            )
            logits = jnp.where(allowed, logits / head_dim**0.5, -1e30)
            grown = jnp.exp(logits - jnp.max(logits, axis=-1, keepdims=True))
            grown = grown / jnp.sum(grown, axis=-1, keepdims=True)
            both.append(jnp.dot(grown.astype(bf16), v, preferred_element_type=f32))
        attended.append(jnp.where(lane < head_dim, both[0], both[1]).astype(bf16))
    attended = jnp.concatenate(attended, axis=1)
    result = jnp.dot(attended, weights[:, 5 * width :], preferred_element_type=f32)
    result = (full + result.astype(bf16).astype(f32)).astype(bf16)
    out[...] = result.reshape(latents, cells, width)


def body(
    level_tokens,
    hidden_probe_match_matrix,
    value_weight,
    pool_out_weight,
    latent_base,
    norm_gain,
    qkv_weight,
    attn_out_weight,
    region_ids,
):
    levels, row_count, col_count, width = level_tokens.shape
    latents, pool_heads, _ = hidden_probe_match_matrix.shape
    lat_count, lon_count = lax.axis_size("lat"), lax.axis_size("lon")
    i, j = lax.axis_index("lat"), lax.axis_index("lon")
    odd = j % 2
    quad = (i // LAT_RING + 2 * (i % LAT_RING)) % LAT_RING

    joined = jnp.concatenate([value_weight, pool_out_weight, qkv_weight, attn_out_weight], axis=1)
    piece_rows, all_columns = joined.shape
    columns = all_columns // (2 * LAT_RING)
    both = lax.dynamic_slice(joined, (0, quad * 2 * columns), (piece_rows, 2 * columns))
    mine = jnp.stack([both[:, :columns], both[:, columns:]])
    mine = jnp.broadcast_to(mine[None], (lon_count // 2, 2, piece_rows, columns))
    mine = mine.reshape(lon_count, piece_rows, columns)
    mine = lax.all_to_all(mine, "lon", 0, 0, tiled=True)
    mine = mine.reshape(lon_count * piece_rows, columns)

    def quarter(rows_at, cols_at):
        part = lax.dynamic_slice(
            level_tokens, (0, rows_at, cols_at, 0), (levels, HALF_LAT, HALF_LON, width)
        )
        return part.reshape(levels, CELLS, width)

    kept, sent = HALF_LAT * (1 - odd), HALF_LAT * odd
    corners = region_ids[::HALF_LAT, ::HALF_LON].reshape(4)
    plane = jnp.repeat(corners.astype(jnp.bfloat16), 4).reshape(1, 16, 1)
    plane = jnp.pad(plane, ((0, 0), (0, CELLS - 16), (0, 0)))
    plane = jnp.broadcast_to(plane, (1, CELLS, width))
    from_band = fetch(jnp.concatenate([quarter(sent, HALF_LON), plane], axis=0), along)
    from_corner = fetch(quarter(kept, 0), across)
    from_east = fetch(quarter(sent, 0), beside)

    parts = [mine] + [fetch(mine, source) for _, source in SLICE_STEPS]
    own_slices = jnp.stack(parts)
    other_slices = fetch(own_slices, other_core)

    theirs = from_band[levels, 0:16:4, 0].astype(jnp.int32)
    corners = jnp.where(odd == 0, corners, theirs)
    window = jnp.where(odd == 0, i, (i + lat_count - 1) % lat_count)
    wraps = (window == lat_count - 1).astype(jnp.int32)
    north = corners[:2] * 2
    south = corners[2:] * 2 + wraps
    labels = jnp.where(
        odd == 0, jnp.concatenate([north, south]), jnp.concatenate([south, north])
    )
    place = jnp.concatenate([jnp.stack([quad, odd]).astype(jnp.int32), labels])
    empty = jnp.zeros((levels, PADDED - 4 * CELLS, width), level_tokens.dtype)
    tokens = jnp.concatenate(
        [quarter(kept, HALF_LON), from_east, from_band[:levels], from_corner, empty], axis=1
    )

    vmem = pl.BlockSpec(memory_space=pltpu.VMEM)
    token_rows = levels * PADDED
    out = pl.pallas_call(
        functools.partial(window_kernel, HEADS, pool_heads),
        out_shape=jax.ShapeDtypeStruct((latents, PADDED, width), jnp.bfloat16),
        in_specs=[pl.BlockSpec(memory_space=pltpu.SMEM)] + [vmem] * 6,
        out_specs=vmem,
        scratch_shapes=[
            pltpu.VMEM((width, all_columns), jnp.bfloat16),
            pltpu.VMEM((token_rows, width), jnp.float32),
        ],
        compiler_params=pltpu.CompilerParams(vmem_limit_bytes=36 * 1024 * 1024),
        name="window",
    )(
        place,
        tokens,
        hidden_probe_match_matrix.reshape(latents * pool_heads, width),
        own_slices,
        other_slices,
        latent_base,
        norm_gain.reshape(1, width),
    )

    def part_of(k):
        return out[:, k * CELLS : (k + 1) * CELLS].reshape(latents, HALF_LAT, HALF_LON, width)

    to_band = give_back(part_of(2), along)
    to_corner = give_back(part_of(3), across)
    to_east = give_back(part_of(1), beside)
    kept_rows = jnp.concatenate([to_corner, part_of(0)], axis=2)
    other_rows = jnp.concatenate([to_east, to_band], axis=2)
    return jnp.where(
        odd == 0,
        jnp.concatenate([other_rows, kept_rows], axis=1),
        jnp.concatenate([kept_rows, other_rows], axis=1),
    )


def solution(mesh):
    placed = (
        P(None, "lat", "lon", None),
        P(),
        P("lon", None),
        P("lon", None),
        P(),
        P(),
        P("lon", None),
        P("lon", None),
        P("lat", "lon"),
    )
    return jax.shard_map(
        body, mesh=mesh, in_specs=placed, out_specs=P(None, "lat", "lon", None), check_vma=False
    )
```

time: 184 us -> 108 us (0.59)
  blocking collectives: 110 us -> 26.1 us
  starting transfers between devices: 23.8 us -> 41.3 us
  matrix products: 13.4 us -> 0 us
  between operations: 13.7 us -> 0.33 us
  waiting for transfers between devices: 11.8 us -> 18.9 us
  Pallas kernels: 0 us -> 5.83 us
  local copies, waits for them, and re-layouts: 8.57 us -> 12.8 us
    all_gather x3 -> x0, blocking collectives: 110 us -> none  [the longest x1 43.3 us: body(): weight_piece = lax.all_gather(value_weight, 'lon', axis=0, tiled=True)]
    all_to_all x0 -> x1, blocking collectives: none -> 26.1 us  [body(): mine = lax.all_to_all(mine, 'lon', 0, 0, tiled=True)]
    ppermute x4 -> x10, starting transfers between devices: 23.8 us -> 41.3 us  [the longest x7 30.4 us: fetch(): return lax.ppermute(block, BOTH, route)]
    dot_general x9 -> x0, matrix products: 11.4 us -> none  [the longest x1 3.29 us: body(): jnp.einsum('mhpd,dhe->mphe', pooled, per_head, preferred_element_type=jnp...]
    ppermute x4 -> x10, waiting for transfers between devices: 11.1 us -> 18.9 us  [the longest x7 17.6 us: fetch(): return lax.ppermute(block, BOTH, route)]
    concatenate x0 -> x1, local copies, waits for them, and re-layouts: none -> 7.56 us  [body(): jnp.concatenate([quarter(kept, HALF_LON), from_east, from_band[:levels],...]
    pallas_call x0 -> x1, Pallas kernels: none -> 5.83 us  [body(): pl.pallas_call(functools.partial(window_kernel, HEADS, pool_heads), out_s...]
    dynamic_update_slice x3 -> x0, local copies, waits for them, and re-layouts: 5.05 us -> none  [body(): pooled = lax.map(pool_one, weights)]
  transfers between devices with their start and end apart: 5 -> 10, of which waited for: 3 -> 6; matrix products, arithmetic and copies ran while one was open for 8% -> 11% of each run, Pallas kernels for 0% -> 0%
where the time goes in v1:
time: 108 us
  starting transfers between devices  41.3 us (38%)
  blocking collectives  26.1 us (24%)
  waiting for transfers between devices  18.9 us (17%)
  local copies, waits for them, and re-layouts  12.8 us (12%)
  Pallas kernels  5.83 us (5%)
  other arithmetic  2.24 us (2%)
    ppermute x7, starting transfers between devices, fetch(): return lax.ppermute(block, BOTH, route)  30.4 us
    all_to_all x1, blocking collectives, body(): mine = lax.all_to_all(mine, 'lon', 0, 0, tiled=True)  26.1 us
    ppermute x7, waiting for transfers between devices, fetch(): return lax.ppermute(block, BOTH, route)  17.6 us
    ppermute x3, starting transfers between devices, give_back(): return lax.ppermute(block, BOTH, [(b, a) for a, b in route])  11 us
    concatenate x1, local copies, waits for them, and re-layouts, body(): jnp.concatenate([quarter(kept, HALF_LON), from_east, from_band[:levels],...  7.56 us
    pallas_call x1, Pallas kernels, body(): pl.pallas_call(functools.partial(window_kernel, HEADS, pool_heads), out_s...  5.83 us
  transfers between devices with their start and end apart: 10, of which 6 were waited for; matrix products, arithmetic and copies ran while one was open for 11% of the time, Pallas kernels for 0%

profile of v1, /device:TPU:1, one launch (start us, length us, event | category | flops | bytes accessed | tf_op | source)
XLA Modules:
  0.0 107.6 jit_solution(3401296733034375988)
XLA Ops:
  0.0 0.7 fusion.2
  0.8 26.1 %all_to_all.5 = bf16[32,16,384]{2,1,0:T(8,128)(2,1)S(1)} all-to-all(bf16[32,16,384]{2,1,0:T(8,128)(2,1)S(1)} %bitcast.26), channel_id=1, replica_groups=mesh['lat'=16,'lon'=32] {'lon'}, dimensions={0} | all-to-all | bytes 786432 | tf_op jit(solution)/shard_map/all_to_all | solution.py:191
  26.9 3.1 %collective-permute-start.5 = (bf16[512,384]{1,0:T(8,128)(2,1)S(1)}, bf16[512,384]{1,0:T(8,128)(2,1)S(1)}, u32[]{:S(2)}, u32[]{:S(2)}) collective-permute-start(bf16[512,384]{1,0:T(8,128)(2,1)S(1)} %bitcast.22), channel_id=1, source_target_pairs={{384,0},{385,1},{386,2},{387,3},{388,4},{389,5},{390,6},{391,7},{3... | collective-permute-start | bytes 1179656 | tf_op jit(solution)/shard_map/ppermute | solution.py:35
  30.1 3.4 %collective-permute-start.4 = (bf16[512,384]{1,0:T(8,128)(2,1)S(1)}, bf16[512,384]{1,0:T(8,128)(2,1)S(1)}, u32[]{:S(2)}, u32[]{:S(2)}) collective-permute-start(bf16[512,384]{1,0:T(8,128)(2,1)S(1)} %bitcast.23), channel_id=1, source_target_pairs={{128,0},{129,1},{130,2},{131,3},{132,4},{133,5},{134,6},{135,7},{1... | collective-permute-start | bytes 1179656 | tf_op jit(solution)/shard_map/ppermute | solution.py:35
  33.4 4.2 %collective-permute-start.3 = (bf16[512,384]{1,0:T(8,128)(2,1)S(1)}, bf16[512,384]{1,0:T(8,128)(2,1)S(1)}, u32[]{:S(2)}, u32[]{:S(2)}) collective-permute-start(bf16[512,384]{1,0:T(8,128)(2,1)S(1)} %bitcast.24), channel_id=1, source_target_pairs={{32,0},{97,1},{34,2},{99,3},{36,4},{101,5},{38,6},{103,7},{40,8},{... | collective-permute-start | bytes 1179656 | tf_op jit(solution)/shard_map/ppermute | solution.py:35
  37.7 2.7 %collective-permute-done.5 = bf16[512,384]{1,0:T(8,128)(2,1)S(1)} collective-permute-done((bf16[512,384]{1,0:T(8,128)(2,1)S(1)}, bf16[512,384]{1,0:T(8,128)(2,1)S(1)}, u32[]{:S(2)}, u32[]{:S(2)}) %collective-permute-start.5) | collective-permute-done | bytes 393248 | tf_op jit(solution)/shard_map/ppermute | solution.py:35
  40.3 1.6 %collective-permute-done.4 = bf16[512,384]{1,0:T(8,128)(2,1)S(1)} collective-permute-done((bf16[512,384]{1,0:T(8,128)(2,1)S(1)}, bf16[512,384]{1,0:T(8,128)(2,1)S(1)}, u32[]{:S(2)}, u32[]{:S(2)}) %collective-permute-start.4) | collective-permute-done | bytes 393248 | tf_op jit(solution)/shard_map/ppermute | solution.py:35
  41.9 3.7 %collective-permute-done.3 = bf16[512,384]{1,0:T(8,128)(2,1)S(1)} collective-permute-done((bf16[512,384]{1,0:T(8,128)(2,1)S(1)}, bf16[512,384]{1,0:T(8,128)(2,1)S(1)}, u32[]{:S(2)}, u32[]{:S(2)}) %collective-permute-start.3) | collective-permute-done | bytes 393248 | tf_op jit(solution)/shard_map/ppermute | solution.py:35
  45.6 0.2 pad_maximum_fusion.own_slices
  45.9 3.6 %collective-permute-start.6 = (bf16[4,512,384]{2,1,0:T(8,128)(2,1)S(1)}, bf16[4,512,384]{2,1,0:T(8,128)(2,1)}, u32[]{:S(2)}, u32[]{:S(2)}) collective-permute-start(bf16[4,512,384]{2,1,0:T(8,128)(2,1)S(1)} %pad_maximum_fusion.own_slices), channel_id=1, source_target_pairs={{1,0},{0,1},{3,2},{2,3},{5,4},{4,5},{7,6},{6,7},{9,8},{8,9},{11,10... | collective-permute-start | bytes 4718600 | tf_op jit(solution)/shard_map/ppermute | solution.py:35
  49.5 0.8 slice.33
  50.3 0.1 reshape.44
  50.4 0.1 broadcast_in_dim.19
  50.5 0.1 reshape_reshape.3
  50.6 0.0 copy-done.3
  50.6 0.1 constant_dynamic-slice_fusion
  50.7 0.1 copy.14
  50.8 0.1 broadcast_in_dim.21
  50.9 4.7 %collective-permute-start = (bf16[14,18,512]{2,1,0:T(8,128)(2,1)S(1)}, bf16[14,18,512]{2,1,0:T(8,128)(2,1)S(1)}, u32[]{:S(2)}, u32[]{:S(2)}) collective-permute-start(bf16[14,18,512]{2,1,0:T(8,128)(2,1)S(1)} %pad_maximum_fusion.1), channel_id=1, source_target_pairs={{32,0},{481,1},{34,2},{483,3},{36,4},{485,5},{38,6},{487,7},{40,8}... | collective-permute-start | bytes 774152 | tf_op jit(solution)/shard_map/ppermute | solution.py:35
  55.6 0.9 copy.15
  56.5 6.7 %collective-permute-start.1 = (bf16[13,18,512]{2,1,0:T(8,128)(2,1)}, bf16[13,18,512]{2,1,0:T(8,128)(2,1)S(1)}, u32[]{:S(2)}, u32[]{:S(2)}) collective-permute-start(bf16[13,18,512]{2,1,0:T(8,128)(2,1)} %copy.15), channel_id=1, source_target_pairs={{1,0},{2,1},{3,2},{4,3},{5,4},{6,5},{7,6},{8,7},{9,8},{10,9},{11,1... | collective-permute-start | bytes 718856 | tf_op jit(solution)/shard_map/ppermute | solution.py:35
  63.2 0.9 copy.16
  64.1 4.6 %collective-permute-start.2 = (bf16[13,18,512]{2,1,0:T(8,128)(2,1)}, bf16[13,18,512]{2,1,0:T(8,128)(2,1)}, u32[]{:S(2)}, u32[]{:S(2)}) collective-permute-start(bf16[13,18,512]{2,1,0:T(8,128)(2,1)} %copy.16), channel_id=1, source_target_pairs={{33,0},{482,1},{35,2},{484,3},{37,4},{486,5},{39,6},{488,7},{41,8}... | collective-permute-start | bytes 718856 | tf_op jit(solution)/shard_map/ppermute | solution.py:35
  68.8 0.1 copy.17
  68.9 0.0 collective-permute-done
  68.9 0.0 copy-start.5
  68.9 0.7 copy-done.5
  69.7 0.0 copy-start.2
  69.7 1.0 slice.44
  70.7 0.0 collective-permute-done.1
  70.8 0.0 copy-start.4
  70.8 9.6 %collective-permute-done.2 = bf16[13,18,512]{2,1,0:T(8,128)(2,1)} collective-permute-done((bf16[13,18,512]{2,1,0:T(8,128)(2,1)}, bf16[13,18,512]{2,1,0:T(8,128)(2,1)}, u32[]{:S(2)}, u32[]{:S(2)}) %collective-permute-start.2) | collective-permute-done | bytes 239648 | tf_op jit(solution)/shard_map/ppermute | solution.py:35
  80.4 7.6 %concatenate.34.tokens = bf16[13,80,512]{2,1,0:T(8,128)(2,1)S(1)} concatenate(bf16[13,18,512]{2,1,0:T(8,128)(2,1)S(1)} %copy.17, bf16[13,18,512]{2,1,0:T(8,128)(2,1)} %copy-done.4, bf16[13,18,512]{2,1,0:T(8,128)(2,1)S(1)} %slice.44, bf16[13,18,512]{2,1,0:T(8,128)(2,1)} %collective-permute-done.2, bf16[13,8,512]{2,1,0:T(8,128)(2,1)S(1)} %broadcast_in_dim.22), dimensions={1} | concatenate | bytes 2129920 | tf_op jit(solution)/shard_map/concatenate | solution.py:224
  87.9 0.1 convert_reduce_fusion
  88.1 0.1 slice_multiply_fusion
  88.1 0.1 broadcast_select_fusion
  88.2 0.1 pad_add_fusion.place
  88.3 0.0 collective-permute-done.6.other_slices
  88.3 0.0 copy-done.1
  88.3 5.8 %window.1 = bf16[3,80,512]{2,1,0:T(8,128)(2,1)S(1)} custom-call(s32[6]{0:T(128)S(1)} %pad_add_fusion.place, bf16[13,80,512]{2,1,0:T(8,128)(2,1)S(1)} %concatenate.34.tokens, bf16[48,512]{1,0:T(8,128)(2,1)S(1)} %bitcast.20, bf16[4,512,384]{2,1,0:T(8,128)(2,1)S(1)} %pad_maximum_fusion.own_slices, bf16[4,512,384]{2,1,0:T(8,128)(2,1)} %collective-permute-done.6.other_slices, ...), custom_call_target="tpu_custom_call" | custom-call | tf_op jit(solution)/shard_map/window/pallas_call | solution.py:230
  94.2 0.1 fusion.3
  94.3 1.9 %collective-permute-start.8 = (bf16[3,3,6,512]{3,2,1,0:T(8,128)(2,1)S(1)}, bf16[3,3,6,512]{3,2,1,0:T(8,128)(2,1)S(1)}, u32[]{:S(2)}, u32[]{:S(2)}) collective-permute-start(bf16[3,3,6,512]{3,2,1,0:T(8,128)(2,1)S(1)} %reshape.54), channel_id=1, source_target_pairs={{0,32},{1,481},{2,34},{3,483},{4,36},{5,485},{6,38},{7,487},{8,40}... | collective-permute-start | bytes 165896 | tf_op jit(solution)/shard_map/ppermute | solution.py:40
  96.3 6.0 %collective-permute-start.9 = (bf16[3,3,6,512]{3,2,1,0:T(8,128)(2,1)S(1)}, bf16[3,3,6,512]{3,2,1,0:T(8,128)(2,1)S(1)}, u32[]{:S(2)}, u32[]{:S(2)}) collective-permute-start(bf16[3,3,6,512]{3,2,1,0:T(8,128)(2,1)S(1)} %reshape.55), channel_id=1, source_target_pairs={{0,33},{1,482},{2,35},{3,484},{4,37},{5,486},{6,39},{7,488},{8,41}... | collective-permute-start | bytes 165896 | tf_op jit(solution)/shard_map/ppermute | solution.py:40
  102.2 3.1 %collective-permute-start.7 = (bf16[3,3,6,512]{3,2,1,0:T(8,128)(2,1)S(1)}, bf16[3,3,6,512]{3,2,1,0:T(8,128)(2,1)S(1)}, u32[]{:S(2)}, u32[]{:S(2)}) collective-permute-start(bf16[3,3,6,512]{3,2,1,0:T(8,128)(2,1)S(1)} %reshape.53), channel_id=1, source_target_pairs={{0,1},{1,2},{2,3},{3,4},{4,5},{5,6},{6,7},{7,8},{8,9},{9,10},{10,1... | collective-permute-start | bytes 165896 | tf_op jit(solution)/shard_map/ppermute | solution.py:40
  105.4 0.0 collective-permute-done.8
  105.4 0.9 collective-permute-done.9
  106.3 0.5 collective-permute-done.7
  106.7 0.8 maximum_select_fusion
  (19 shorter events, 0.3 us)
Async XLA Ops:
  26.9 13.4 %collective-permute-start.5 = (bf16[512,384]{1,0:T(8,128)(2,1)S(1)}, bf16[512,384]{1,0:T(8,128)(2,1)S(1)}, u32[]{:S(2)}, u32[]{:S(2)}) collective-permute-start(bf16[512,384]{1,0:T(8,128)(2,1)S(1)} %bitcast.22), channel_id=1, source_target_pairs={{384,0},{385,1},{386,2},{387,3},{388,4},{389,5},{390,6},{391,7},{3... | collective-permute-start | bytes 1179656 | tf_op jit(solution)/shard_map/ppermute | solution.py:35
  30.1 11.9 %collective-permute-start.4 = (bf16[512,384]{1,0:T(8,128)(2,1)S(1)}, bf16[512,384]{1,0:T(8,128)(2,1)S(1)}, u32[]{:S(2)}, u32[]{:S(2)}) collective-permute-start(bf16[512,384]{1,0:T(8,128)(2,1)S(1)} %bitcast.23), channel_id=1, source_target_pairs={{128,0},{129,1},{130,2},{131,3},{132,4},{133,5},{134,6},{135,7},{1... | collective-permute-start | bytes 1179656 | tf_op jit(solution)/shard_map/ppermute | solution.py:35
  33.4 12.2 %collective-permute-start.3 = (bf16[512,384]{1,0:T(8,128)(2,1)S(1)}, bf16[512,384]{1,0:T(8,128)(2,1)S(1)}, u32[]{:S(2)}, u32[]{:S(2)}) collective-permute-start(bf16[512,384]{1,0:T(8,128)(2,1)S(1)} %bitcast.24), channel_id=1, source_target_pairs={{32,0},{97,1},{34,2},{99,3},{36,4},{101,5},{38,6},{103,7},{40,8},{... | collective-permute-start | bytes 1179656 | tf_op jit(solution)/shard_map/ppermute | solution.py:35
  45.6 4.9 %copy-start.3 = (bf16[13,6,12,512]{3,0,2,1:T(8,128)(2,1)S(1)}, bf16[13,6,12,512]{3,0,2,1:T(8,128)(2,1)}, u32[]{:S(2)}) copy-start(bf16[13,6,12,512]{3,0,2,1:T(8,128)(2,1)} %param.9) | copy-start | bytes 2875396
  45.9 42.4 %collective-permute-start.6 = (bf16[4,512,384]{2,1,0:T(8,128)(2,1)S(1)}, bf16[4,512,384]{2,1,0:T(8,128)(2,1)}, u32[]{:S(2)}, u32[]{:S(2)}) collective-permute-start(bf16[4,512,384]{2,1,0:T(8,128)(2,1)S(1)} %pad_maximum_fusion.own_slices), channel_id=1, source_target_pairs={{1,0},{0,1},{3,2},{2,3},{5,4},{4,5},{7,6},{6,7},{9,8},{8,9},{11,10... | collective-permute-start | bytes 4718600 | tf_op jit(solution)/shard_map/ppermute | solution.py:35
  50.9 18.0 %collective-permute-start = (bf16[14,18,512]{2,1,0:T(8,128)(2,1)S(1)}, bf16[14,18,512]{2,1,0:T(8,128)(2,1)S(1)}, u32[]{:S(2)}, u32[]{:S(2)}) collective-permute-start(bf16[14,18,512]{2,1,0:T(8,128)(2,1)S(1)} %pad_maximum_fusion.1), channel_id=1, source_target_pairs={{32,0},{481,1},{34,2},{483,3},{36,4},{485,5},{38,6},{487,7},{40,8}... | collective-permute-start | bytes 774152 | tf_op jit(solution)/shard_map/ppermute | solution.py:35
  56.5 14.2 %collective-permute-start.1 = (bf16[13,18,512]{2,1,0:T(8,128)(2,1)}, bf16[13,18,512]{2,1,0:T(8,128)(2,1)S(1)}, u32[]{:S(2)}, u32[]{:S(2)}) collective-permute-start(bf16[13,18,512]{2,1,0:T(8,128)(2,1)} %copy.15), channel_id=1, source_target_pairs={{1,0},{2,1},{3,2},{4,3},{5,4},{6,5},{7,6},{8,7},{9,8},{10,9},{11,1... | collective-permute-start | bytes 718856 | tf_op jit(solution)/shard_map/ppermute | solution.py:35
  64.1 16.3 %collective-permute-start.2 = (bf16[13,18,512]{2,1,0:T(8,128)(2,1)}, bf16[13,18,512]{2,1,0:T(8,128)(2,1)}, u32[]{:S(2)}, u32[]{:S(2)}) collective-permute-start(bf16[13,18,512]{2,1,0:T(8,128)(2,1)} %copy.16), channel_id=1, source_target_pairs={{33,0},{482,1},{35,2},{484,3},{37,4},{486,5},{39,6},{488,7},{41,8}... | collective-permute-start | bytes 718856 | tf_op jit(solution)/shard_map/ppermute | solution.py:35
  68.9 0.7 copy-start.5
  69.7 18.6 %copy-start = (bf16[3,16,512]{2,1,0:T(8,128)(2,1)S(1)}, bf16[3,16,512]{2,1,0:T(8,128)(2,1)}, u32[]{:S(2)}) copy-start(bf16[3,16,512]{2,1,0:T(8,128)(2,1)} %param.10) | copy-start | bytes 147460
  69.7 18.6 %copy-start.1 = (bf16[3,512]{1,0:T(4,128)(2,1)S(1)}, bf16[3,512]{1,0:T(4,128)(2,1)}, u32[]{:S(2)}) copy-start(bf16[3,512]{1,0:T(4,128)(2,1)} %base.1) | copy-start | bytes 9220
  69.7 18.6 %copy-start.2 = (f32[512]{0:T(512)S(1)}, f32[512]{0:T(512)}, u32[]{:S(2)}) copy-start(f32[512]{0:T(512)} %param.14) | copy-start | bytes 6148
  70.8 9.6 %copy-start.4 = (bf16[13,18,512]{2,1,0:T(8,128)(2,1)}, bf16[13,18,512]{2,1,0:T(8,128)(2,1)S(1)}, u32[]{:S(2)}) copy-start(bf16[13,18,512]{2,1,0:T(8,128)(2,1)S(1)} %collective-permute-done.1) | copy-start | bytes 718852
  94.3 11.0 %collective-permute-start.8 = (bf16[3,3,6,512]{3,2,1,0:T(8,128)(2,1)S(1)}, bf16[3,3,6,512]{3,2,1,0:T(8,128)(2,1)S(1)}, u32[]{:S(2)}, u32[]{:S(2)}) collective-permute-start(bf16[3,3,6,512]{3,2,1,0:T(8,128)(2,1)S(1)} %reshape.54), channel_id=1, source_target_pairs={{0,32},{1,481},{2,34},{3,483},{4,36},{5,485},{6,38},{7,487},{8,40}... | collective-permute-start | bytes 165896 | tf_op jit(solution)/shard_map/ppermute | solution.py:40
  96.3 10.0 %collective-permute-start.9 = (bf16[3,3,6,512]{3,2,1,0:T(8,128)(2,1)S(1)}, bf16[3,3,6,512]{3,2,1,0:T(8,128)(2,1)S(1)}, u32[]{:S(2)}, u32[]{:S(2)}) collective-permute-start(bf16[3,3,6,512]{3,2,1,0:T(8,128)(2,1)S(1)} %reshape.55), channel_id=1, source_target_pairs={{0,33},{1,482},{2,35},{3,484},{4,37},{5,486},{6,39},{7,488},{8,41}... | collective-permute-start | bytes 165896 | tf_op jit(solution)/shard_map/ppermute | solution.py:40
  102.2 4.5 %collective-permute-start.7 = (bf16[3,3,6,512]{3,2,1,0:T(8,128)(2,1)S(1)}, bf16[3,3,6,512]{3,2,1,0:T(8,128)(2,1)S(1)}, u32[]{:S(2)}, u32[]{:S(2)}) collective-permute-start(bf16[3,3,6,512]{3,2,1,0:T(8,128)(2,1)S(1)} %reshape.53), channel_id=1, source_target_pairs={{0,1},{1,2},{2,3},{3,4},{4,5},{5,6},{6,7},{7,8},{8,9},{9,10},{10,1... | collective-permute-start | bytes 165896 | tf_op jit(solution)/shard_map/ppermute | solution.py:40

commit v2 on v1

v2 whole, which is shorter than its diff:
```python
import functools

import jax
import jax.numpy as jnp
from jax import lax
from jax.experimental import pallas as pl
from jax.experimental.pallas import tpu as pltpu
from jax.sharding import PartitionSpec as P

HEADS = 8
LATENTS = 3
WIN_LAT = 6
WIN_LON = 12
HALF_LAT = WIN_LAT // 2
HALF_LON = WIN_LON // 2
CELLS = HALF_LAT * HALF_LON
PADDED = 80
LAT_RING = 4
STABILIZER_TINY = 1e-05
BOTH = ("lat", "lon")
LIMIT = 24 * 1024 * 1024


def pairs(source_of, lat_count, lon_count):
    route = []
    for i in range(lat_count):
        for j in range(lon_count):
            si, sj = source_of(i, j)
            source = (si % lat_count) * lon_count + sj % lon_count
            route.append((source, i * lon_count + j))
    return route


def fetch(block, source_of):
    route = pairs(source_of, lax.axis_size("lat"), lax.axis_size("lon"))
    return lax.ppermute(block, BOTH, route)


def give_back(block, source_of):
    route = pairs(source_of, lax.axis_size("lat"), lax.axis_size("lon"))
    return lax.ppermute(block, BOTH, [(b, a) for a, b in route])


def band_of(j):
    return 1 if j % 2 == 0 else -1


def beside(i, j):
    return i, j + 1


def along(i, j):
    return i + band_of(j), j


def across(i, j):
    return i + band_of(j), j + 1


def next_along_x(i, j):
    return i + band_of(j) * LAT_RING, j


def other_core(i, j):
    return i, j + 1 if j % 2 == 0 else j - 1


def quarter_kernel(place, regions, far_tokens, own, east, band, corner, tokens, rows, arrived):
    levels = tokens.shape[0]
    copies = [
        pltpu.make_async_copy(far_tokens.at[level], tokens.at[level], arrived.at[level])
        for level in range(levels)
    ]
    for copy in copies:
        copy.start()
    odd = place[1]
    kept, sent = HALF_LAT * (1 - odd), HALF_LAT * odd
    for k in range(4):
        label = regions[HALF_LAT * (k // 2), HALF_LON * (k % 2)]
        label = jnp.full((1, rows.shape[1]), label, jnp.int32)
        rows[levels * CELLS + k : levels * CELLS + k + 1] = label.astype(jnp.float32)
    rows[levels * CELLS + 4 :] = jnp.zeros((2, rows.shape[1]), jnp.float32)
    for n, (out, top, left) in enumerate(
        ((band, sent, HALF_LON), (corner, kept, 0), (east, sent, 0), (own, kept, HALF_LON))
    ):
        for level in range(levels):
            if n == 0:
                copies[level].wait()
            for r in range(HALF_LAT):
                row = tokens[level, top + r].astype(jnp.float32)
                at = level * CELLS + r * HALF_LON
                rows[at : at + HALF_LON] = row[left : left + HALF_LON]
        out[...] = rows[...].astype(out.dtype)


def mix_kernel(levels, place, own, east, band, corner, probe, tokens, mix, labels, joined):
    width = own.shape[1]
    cells = PADDED
    for k, part in enumerate((own, east, band, corner)):
        rows = part[...].astype(jnp.float32)
        for level in range(levels):
            joined[level, k * CELLS : (k + 1) * CELLS] = rows[level * CELLS : (level + 1) * CELLS]
    joined[:, 4 * CELLS :] = jnp.zeros((levels, cells - 4 * CELLS, width), jnp.float32)
    x = joined[...].astype(jnp.bfloat16).reshape(levels * cells, width)
    tokens[...] = x
    scores = lax.dot_general(
        x, probe[...], (((1,), (1,)), ((), ())), preferred_element_type=jnp.float32
    )
    scores = scores.reshape(levels, cells, probe.shape[0])
    scores = jnp.exp(scores - jnp.max(scores, axis=0, keepdims=True))
    weights = scores / jnp.sum(scores, axis=0, keepdims=True)
    mix[...] = weights.astype(jnp.bfloat16).reshape(levels * cells, probe.shape[0])
    at = levels * CELLS
    near = own[...].astype(jnp.float32)[at : at + 4, :128]
    far = band[...].astype(jnp.float32)[at : at + 4, :128]
    odd = jnp.full((4, 128), place[1], jnp.int32)
    ids = 2.0 * jnp.where(odd == 0, near, far)
    north = ids[:2]
    south = ids[2:] + jnp.full((2, 128), place[2], jnp.int32).astype(jnp.float32)
    first = odd[:2] == 0
    labels[:2] = jnp.where(first, north, south)
    labels[2:4] = jnp.where(first, south, north)
    labels[4:] = jnp.zeros((4, 128), jnp.float32)


def window_kernel(
    heads,
    pool_heads,
    place,
    tokens,
    mix,
    mine,
    ahead,
    mine_swapped,
    ahead_swapped,
    labels,
    base,
    gain,
    out,
    weights,
    values,
):
    latents, width = base.shape
    cells = PADDED
    level_count = tokens.shape[0] // cells
    columns = mine.shape[1]
    f32 = jnp.float32
    bf16 = jnp.bfloat16
    parity, core = place[0], place[1]
    for ref, group, side in (
        (mine, parity, core),
        (ahead, 1 - parity, core),
        (mine_swapped, parity, 1 - core),
        (ahead_swapped, 1 - parity, 1 - core),
    ):
        start = (group * 2 + side) * columns
        weights[:, pl.ds(pl.multiple_of(start, 128), columns)] = ref[...]

    values[...] = jnp.dot(tokens[...], weights[:, :width], preferred_element_type=f32)
    span = width // pool_heads
    head_of = lax.broadcasted_iota(jnp.int32, (latents * pool_heads, width), 1) // span
    row_of = lax.broadcasted_iota(jnp.int32, (latents * pool_heads, width), 0)
    pooled = []
    for m in range(latents):
        spread = jnp.where(row_of == head_of + m * pool_heads, 1.0, 0.0).astype(bf16)
        share = jnp.dot(mix[...], spread, preferred_element_type=f32) * values[...]
        pooled.append(jnp.sum(share.reshape(level_count, cells, width), axis=0).astype(bf16))
    pooled = jnp.concatenate(pooled, axis=0)
    latent = jnp.dot(pooled, weights[:, width : 2 * width], preferred_element_type=f32)
    base_rows = jnp.broadcast_to(base[...].astype(f32)[:, None, :], (latents, cells, width))
    latent = (latent + base_rows.reshape(latents * cells, width)).astype(bf16)

    full = latent.astype(f32)
    centred = full - jnp.mean(full, axis=-1, keepdims=True)
    variance = jnp.mean(centred * centred, axis=-1, keepdims=True)
    normed = (centred * lax.rsqrt(variance + STABILIZER_TINY) * gain[...]).astype(bf16)
    qkv = jnp.dot(normed, weights[:, 2 * width : 5 * width], preferred_element_type=f32)
    qkv = qkv.astype(bf16)

    tokens_in = latents * cells
    quarter_labels = [labels[k : k + 1, 0:1] for k in range(4)]

    def labels_of(shape, axis):
        cell = lax.rem(lax.broadcasted_iota(jnp.int32, shape, axis), cells)
        label = jnp.full(shape, -1.0, jnp.float32)
        for k in range(3, -1, -1):
            label = jnp.where(
                cell < CELLS * (k + 1), jnp.broadcast_to(quarter_labels[k], shape), label
            )
        return label

    allowed = labels_of((tokens_in, 1), 0) == labels_of((1, tokens_in), 1)
    head_dim = width // heads
    pair = 2 * head_dim
    lane = lax.broadcasted_iota(jnp.int32, (1, pair), 1)
    left = jnp.where(lane < head_dim, 1.0, 0.0)
    sides = (left.astype(bf16), (1.0 - left).astype(bf16))
    attended = []
    for h in range(heads // 2):
        q = qkv[:, h * pair : (h + 1) * pair]
        k = qkv[:, width + h * pair : width + (h + 1) * pair]
        v = qkv[:, 2 * width + h * pair : 2 * width + (h + 1) * pair]
        both = []
        for side in sides:
            logits = lax.dot_general(
                q * side, k, (((1,), (1,)), ((), ())), preferred_element_type=f32
            )
            logits = jnp.where(allowed, logits / head_dim**0.5, -1e30)
            grown = jnp.exp(logits - jnp.max(logits, axis=-1, keepdims=True))
            grown = grown / jnp.sum(grown, axis=-1, keepdims=True)
            both.append(jnp.dot(grown.astype(bf16), v, preferred_element_type=f32))
        attended.append(jnp.where(lane < head_dim, both[0], both[1]).astype(bf16))
    attended = jnp.concatenate(attended, axis=1)
    result = jnp.dot(attended, weights[:, 5 * width :], preferred_element_type=f32)
    result = (full + result.astype(bf16).astype(f32)).astype(bf16)
    out[...] = result.reshape(latents, cells, width)


def body(
    level_tokens,
    hidden_probe_match_matrix,
    value_weight,
    pool_out_weight,
    latent_base,
    norm_gain,
    qkv_weight,
    attn_out_weight,
    region_ids,
):
    levels, row_count, col_count, width = level_tokens.shape
    latents, pool_heads, _ = hidden_probe_match_matrix.shape
    lat_count, lon_count = lax.axis_size("lat"), lax.axis_size("lon")
    i, j = lax.axis_index("lat"), lax.axis_index("lon")
    odd = j % 2
    parity = (i // LAT_RING) % 2

    joined = jnp.concatenate([value_weight, pool_out_weight, qkv_weight, attn_out_weight], axis=1)
    piece_rows, all_columns = joined.shape
    columns = all_columns // 4
    both = lax.dynamic_slice(joined, (0, parity * 2 * columns), (piece_rows, 2 * columns))
    mine = jnp.stack([both[:, :columns], both[:, columns:]])
    mine = jnp.broadcast_to(mine[None], (lon_count // 2, 2, piece_rows, columns))
    mine = mine.reshape(lon_count, piece_rows, columns)
    mine = lax.all_to_all(mine, "lon", 0, 0, tiled=True)
    mine = mine.reshape(lon_count * piece_rows, columns)

    vmem = pl.BlockSpec(memory_space=pltpu.VMEM)
    smem = pl.BlockSpec(memory_space=pltpu.SMEM)
    window = jnp.where(odd == 0, i, (i + lat_count - 1) % lat_count)
    place = jnp.stack([parity, odd, (window == lat_count - 1).astype(jnp.int32)]).astype(jnp.int32)
    packed = levels * CELLS + 6
    quarter = jax.ShapeDtypeStruct((packed, width), level_tokens.dtype)
    own, east, band, corner = pl.pallas_call(
        quarter_kernel,
        out_shape=[quarter] * 4,
        in_specs=[smem, smem, pl.BlockSpec(memory_space=pl.ANY)],
        out_specs=[vmem] * 4,
        scratch_shapes=[
            pltpu.VMEM(level_tokens.shape, level_tokens.dtype),
            pltpu.VMEM((packed, width), jnp.float32),
            pltpu.SemaphoreType.DMA((levels,)),
        ],
        compiler_params=pltpu.CompilerParams(vmem_limit_bytes=LIMIT),
        name="quarters",
    )(place, region_ids, level_tokens)
    band = fetch(band, along)
    corner = fetch(corner, across)
    mine, band, corner, east = lax.optimization_barrier((mine, band, corner, east))
    ahead = fetch(mine, next_along_x)
    east = fetch(east, beside)

    again, east = lax.optimization_barrier((mine, east))
    mine_swapped = fetch(again, other_core)
    ahead, east = lax.optimization_barrier((ahead, east))
    token_rows = levels * PADDED
    mixes = latents * pool_heads
    tokens, mix, labels = pl.pallas_call(
        functools.partial(mix_kernel, levels),
        out_shape=[
            jax.ShapeDtypeStruct((token_rows, width), jnp.bfloat16),
            jax.ShapeDtypeStruct((token_rows, mixes), jnp.bfloat16),
            jax.ShapeDtypeStruct((8, 128), jnp.float32),
        ],
        in_specs=[smem] + [vmem] * 5,
        out_specs=[vmem] * 3,
        scratch_shapes=[pltpu.VMEM((levels, PADDED, width), jnp.float32)],
        compiler_params=pltpu.CompilerParams(vmem_limit_bytes=LIMIT),
        cost_estimate=pl.CostEstimate(
            flops=2 * token_rows * width * mixes, bytes_accessed=8 << 20, transcendentals=0
        ),
        name="mix",
    )(place, own, east, band, corner, hidden_probe_match_matrix.reshape(mixes, width))

    ahead_swapped = fetch(ahead, other_core)
    out = pl.pallas_call(
        functools.partial(window_kernel, HEADS, pool_heads),
        out_shape=jax.ShapeDtypeStruct((latents, PADDED, width), jnp.bfloat16),
        in_specs=[smem] + [vmem] * 9,
        out_specs=vmem,
        scratch_shapes=[
            pltpu.VMEM((width, all_columns), jnp.bfloat16),
            pltpu.VMEM((token_rows, width), jnp.float32),
        ],
        compiler_params=pltpu.CompilerParams(vmem_limit_bytes=LIMIT),
        name="window",
    )(
        place,
        tokens,
        mix,
        mine,
        ahead,
        mine_swapped,
        ahead_swapped,
        labels,
        latent_base,
        norm_gain.reshape(1, width),
    )

    def part_of(k):
        return out[:, k * CELLS : (k + 1) * CELLS].reshape(latents, HALF_LAT, HALF_LON, width)

    to_band = give_back(part_of(2), along)
    to_corner = give_back(part_of(3), across)
    to_east = give_back(part_of(1), beside)
    kept_rows = jnp.concatenate([to_corner, part_of(0)], axis=2)
    other_rows = jnp.concatenate([to_east, to_band], axis=2)
    return jnp.where(
        odd == 0,
        jnp.concatenate([other_rows, kept_rows], axis=1),
        jnp.concatenate([kept_rows, other_rows], axis=1),
    )


def solution(mesh):
    placed = (
        P(None, "lat", "lon", None),
        P(),
        P("lon", None),
        P("lon", None),
        P(),
        P(),
        P("lon", None),
        P("lon", None),
        P("lat", "lon"),
    )
    return jax.shard_map(
        body, mesh=mesh, in_specs=placed, out_specs=P(None, "lat", "lon", None), check_vma=False
    )
```

time: 108 us -> 80.8 us (0.75)
  blocking collectives: 26.1 us -> 0 us
  local copies, waits for them, and re-layouts: 12.8 us -> 1.75 us
  waiting for transfers between devices: 18.9 us -> 23.2 us
  starting transfers between devices: 41.3 us -> 44.8 us
  Pallas kernels: 5.83 us -> 8.47 us
    all_to_all x1 -> x0, blocking collectives: 26.1 us -> none  [body(): mine = lax.all_to_all(mine, 'lon', 0, 0, tiled=True)]
    all_to_all x0 -> x1, starting transfers between devices: none -> 13 us  [body(): mine = lax.all_to_all(mine, 'lon', 0, 0, tiled=True)]
    ppermute x7 -> x6, starting transfers between devices: 30.4 us -> 19 us  [fetch(): return lax.ppermute(block, BOTH, route)]
    concatenate x1 -> x0, local copies, waits for them, and re-layouts: 7.56 us -> none  [body(): jnp.concatenate([quarter(kept, HALF_LON), from_east, from_band[:levels],...]
    ppermute x7 -> x6, waiting for transfers between devices: 17.6 us -> 21.6 us  [fetch(): return lax.ppermute(block, BOTH, route)]
    pallas_call x0 -> x2, Pallas kernels: none -> 3.96 us  [the longest x1 2.78 us: body(): pl.pallas_call(quarter_kernel, out_shape=[quarter] * 4, in_specs=[smem, s...]
    reshape x5 -> x0, local copies, waits for them, and re-layouts: 2.14 us -> none  [the longest x4 2.06 us: quarter(): return part.reshape(levels, CELLS, width)]
    ppermute x3, starting transfers between devices: 11 us -> 12.8 us  [give_back(): return lax.ppermute(block, BOTH, [(b, a) for a, b in route])]
  transfers between devices with their start and end apart: 10 -> 10, of which waited for: 6 -> 6; matrix products, arithmetic and copies ran while one was open for 11% -> 1% of each run, Pallas kernels for 0% -> 5%
where the time goes in v2:
time: 80.8 us; the launch traced here: 80.3 us
  starting transfers between devices  44.8 us (55%)
  waiting for transfers between devices  23.2 us (29%)
  Pallas kernels  8.47 us (10%)
  local copies, waits for them, and re-layouts  1.75 us (2%)
  other arithmetic  1.72 us (2%)
    ppermute x6, waiting for transfers between devices, fetch(): return lax.ppermute(block, BOTH, route)  21.6 us
    ppermute x6, starting transfers between devices, fetch(): return lax.ppermute(block, BOTH, route)  19 us
    all_to_all x1, starting transfers between devices, body(): mine = lax.all_to_all(mine, 'lon', 0, 0, tiled=True)  13 us
    ppermute x3, starting transfers between devices, give_back(): return lax.ppermute(block, BOTH, [(b, a) for a, b in route])  12.8 us
    pallas_call x1, Pallas kernels, body(): pl.pallas_call(functools.partial(window_kernel, HEADS, pool_heads), out_s...  4.52 us
    pallas_call x1, Pallas kernels, body(): pl.pallas_call(quarter_kernel, out_shape=[quarter] * 4, in_specs=[smem, s...  2.78 us
    ppermute x3, waiting for transfers between devices, give_back(): return lax.ppermute(block, BOTH, [(b, a) for a, b in route])  1.62 us
  transfers between devices with their start and end apart: 10, of which 6 were waited for; matrix products, arithmetic and copies ran while one was open for 1% of the time, Pallas kernels for 5%

profile of v2, /device:TPU:1, one launch (start us, length us, event | category | flops | bytes accessed | tf_op | source)
XLA Modules:
  0.0 80.3 jit_solution(18338438520720102666)
XLA Ops:
  0.0 0.8 fusion.2
  0.8 0.0 copy-start.4
  0.8 1.0 %broadcast_in_dim.2 = bf16[16,2,16,768]{3,2,1,0:T(8,128)(2,1)} broadcast(bf16[2,16,768]{2,1,0:T(8,128)(2,1)S(1)} %pad_maximum_fusion), dimensions={1,2,3} | broadcast | bytes 835584 | tf_op jit(solution)/shard_map/broadcast_in_dim | solution.py:242
  1.8 13.0 %all-to-all-start = ((bf16[32,16,768]{2,1,0:T(8,128)(2,1)}), bf16[32,16,768]{2,1,0:T(8,128)(2,1)S(1)}, u32[]{:S(2)}, u32[]{:S(2)}) async-start(bf16[32,16,768]{2,1,0:T(8,128)(2,1)} %bitcast.5), calls=%async_computation | async-start | bytes 1572864 | tf_op jit(solution)/shard_map/all_to_all | solution.py:244
  14.8 0.0 copy-done.4
  14.8 0.0 copy-start.1
  14.9 0.6 copy.10.far_tokens
  15.4 0.0 copy-start
  15.5 0.0 copy-start.2
  15.5 0.0 copy-start.3
  15.5 0.1 pad_add_fusion.place
  15.6 0.0 copy-done.1
  15.6 2.8 %quarters.1 = (bf16[240,512]{1,0:T(8,128)(2,1)S(1)}, bf16[240,512]{1,0:T(8,128)(2,1)S(1)}, bf16[240,512]{1,0:T(8,128)(2,1)S(1)}, bf16[240,512]{1,0:T(8,128)(2,1)S(1)}) custom-call(s32[3]{0:T(128)S(1)} %pad_add_fusion.place, s32[6,12]{1,0:T(8,128)S(1)} %copy-done.1, bf16[13,6,12,512]{3,2,1,0:T(8,128)(2,1)S(1)} %copy.10.far_tokens), custom_call_target="tpu_custom_call" | custom-call | tf_op jit(solution)/shard_map/quarters/pallas_call | solution.py:253
  18.4 4.2 %collective-permute-start = (bf16[240,512]{1,0:T(8,128)(2,1)S(1)}, bf16[240,512]{1,0:T(8,128)(2,1)S(1)}, u32[]{:S(2)}, u32[]{:S(2)}) collective-permute-start(bf16[240,512]{1,0:T(8,128)(2,1)S(1)} %get-tuple-element.21), channel_id=1, source_target_pairs={{32,0},{481,1},{34,2},{483,3},{36,4},{485,5},{38,6},{487,7},{40,8}... | collective-permute-start | bytes 737288 | tf_op jit(solution)/shard_map/ppermute | solution.py:36
  22.6 7.1 %collective-permute-start.1 = (bf16[240,512]{1,0:T(8,128)(2,1)S(1)}, bf16[240,512]{1,0:T(8,128)(2,1)S(1)}, u32[]{:S(2)}, u32[]{:S(2)}) collective-permute-start(bf16[240,512]{1,0:T(8,128)(2,1)S(1)} %get-tuple-element.22), channel_id=1, source_target_pairs={{33,0},{482,1},{35,2},{484,3},{37,4},{486,5},{39,6},{488,7},{41,8}... | collective-permute-start | bytes 737288 | tf_op jit(solution)/shard_map/ppermute | solution.py:36
  29.7 7.7 %collective-permute-done.band = bf16[240,512]{1,0:T(8,128)(2,1)S(1)} collective-permute-done((bf16[240,512]{1,0:T(8,128)(2,1)S(1)}, bf16[240,512]{1,0:T(8,128)(2,1)S(1)}, u32[]{:S(2)}, u32[]{:S(2)}) %collective-permute-start) | collective-permute-done | bytes 245792 | tf_op jit(solution)/shard_map/ppermute | solution.py:36
  37.5 4.7 %collective-permute-done.1.corner = bf16[240,512]{1,0:T(8,128)(2,1)S(1)} collective-permute-done((bf16[240,512]{1,0:T(8,128)(2,1)S(1)}, bf16[240,512]{1,0:T(8,128)(2,1)S(1)}, u32[]{:S(2)}, u32[]{:S(2)}) %collective-permute-start.1) | collective-permute-done | bytes 245792 | tf_op jit(solution)/shard_map/ppermute | solution.py:36
  42.2 0.0 all-to-all-done
  42.2 1.9 %collective-permute-start.2 = (bf16[512,768]{1,0:T(8,128)(2,1)S(1)}, bf16[512,768]{1,0:T(8,128)(2,1)S(1)}, u32[]{:S(2)}, u32[]{:S(2)}) collective-permute-start(bf16[512,768]{1,0:T(8,128)(2,1)S(1)} %bitcast.11), channel_id=1, source_target_pairs={{128,0},{385,1},{130,2},{387,3},{132,4},{389,5},{134,6},{391,7},{1... | collective-permute-start | bytes 2359304 | tf_op jit(solution)/shard_map/ppermute | solution.py:36
  44.1 1.9 %collective-permute-start.3 = (bf16[240,512]{1,0:T(8,128)(2,1)S(1)}, bf16[240,512]{1,0:T(8,128)(2,1)S(1)}, u32[]{:S(2)}, u32[]{:S(2)}) collective-permute-start(bf16[240,512]{1,0:T(8,128)(2,1)S(1)} %get-tuple-element.25), channel_id=1, source_target_pairs={{1,0},{2,1},{3,2},{4,3},{5,4},{6,5},{7,6},{8,7},{9,8},{10,9},{11,1... | collective-permute-start | bytes 737288 | tf_op jit(solution)/shard_map/ppermute | solution.py:36
  46.0 5.9 %collective-permute-done.3.east = bf16[240,512]{1,0:T(8,128)(2,1)S(1)} collective-permute-done((bf16[240,512]{1,0:T(8,128)(2,1)S(1)}, bf16[240,512]{1,0:T(8,128)(2,1)S(1)}, u32[]{:S(2)}, u32[]{:S(2)}) %collective-permute-start.3) | collective-permute-done | bytes 245792 | tf_op jit(solution)/shard_map/ppermute | solution.py:36
  51.9 2.0 %collective-permute-start.4 = (bf16[512,768]{1,0:T(8,128)(2,1)S(1)}, bf16[512,768]{1,0:T(8,128)(2,1)S(1)}, u32[]{:S(2)}, u32[]{:S(2)}) collective-permute-start(bf16[512,768]{1,0:T(8,128)(2,1)S(1)} %bitcast.12), channel_id=1, source_target_pairs={{1,0},{0,1},{3,2},{2,3},{5,4},{4,5},{7,6},{6,7},{9,8},{8,9},{11,10... | collective-permute-start | bytes 2359304 | tf_op jit(solution)/shard_map/ppermute | solution.py:36
  53.9 2.2 %collective-permute-done.2.ahead = bf16[512,768]{1,0:T(8,128)(2,1)S(1)} collective-permute-done((bf16[512,768]{1,0:T(8,128)(2,1)S(1)}, bf16[512,768]{1,0:T(8,128)(2,1)S(1)}, u32[]{:S(2)}, u32[]{:S(2)}) %collective-permute-start.2) | collective-permute-done | bytes 786464 | tf_op jit(solution)/shard_map/ppermute | solution.py:36
  56.1 1.9 %collective-permute-start.5 = (bf16[512,768]{1,0:T(8,128)(2,1)S(1)}, bf16[512,768]{1,0:T(8,128)(2,1)S(1)}, u32[]{:S(2)}, u32[]{:S(2)}) collective-permute-start(bf16[512,768]{1,0:T(8,128)(2,1)S(1)} %collective-permute-done.2.ahead), channel_id=1, source_target_pairs={{1,0},{0,1},{3,2},{2,3},{5,4},{4,5},{7,6},{6,7},{9,8},{8,9},{11,10... | collective-permute-start | bytes 2359304 | tf_op jit(solution)/shard_map/ppermute | solution.py:36
  58.0 0.0 copy-done
  58.0 1.2 %mix.1 = (bf16[1040,512]{1,0:T(8,128)(2,1)S(1)}, bf16[1040,48]{1,0:T(8,128)(2,1)S(1)}, f32[8,128]{1,0:T(8,128)S(1)}) custom-call(s32[3]{0:T(128)S(1)} %pad_add_fusion.place, bf16[240,512]{1,0:T(8,128)(2,1)S(1)} %get-tuple-element.20.own, bf16[240,512]{1,0:T(8,128)(2,1)S(1)} %collective-permute-done.3.east, bf16[240,512]{1,0:T(8,128)(2,1)S(1)} %collective-permute-done.band, ...), custom_call_target="tpu_custom_call" | custom-call | flops 51118080 | bytes 8388608 | tf_op jit(solution)/shard_map/mix/pallas_call | solution.py:277
  59.2 0.0 collective-permute-done.4.mine_swapped
  59.2 1.0 %collective-permute-done.5.ahead_swapped = bf16[512,768]{1,0:T(8,128)(2,1)S(1)} collective-permute-done((bf16[512,768]{1,0:T(8,128)(2,1)S(1)}, bf16[512,768]{1,0:T(8,128)(2,1)S(1)}, u32[]{:S(2)}, u32[]{:S(2)}) %collective-permute-start.5) | collective-permute-done | bytes 786464 | tf_op jit(solution)/shard_map/ppermute | solution.py:36
  60.3 0.0 copy-done.2
  60.3 0.0 copy-done.3
  60.3 4.5 %window.1 = bf16[3,80,512]{2,1,0:T(8,128)(2,1)S(1)} custom-call(s32[3]{0:T(128)S(1)} %pad_add_fusion.place, bf16[1040,512]{1,0:T(8,128)(2,1)S(1)} %get-tuple-element.30.tokens, bf16[1040,48]{1,0:T(8,128)(2,1)S(1)} %get-tuple-element.31.mix, bf16[512,768]{1,0:T(8,128)(2,1)S(1)} %bitcast.13, bf16[512,768]{1,0:T(8,128)(2,1)S(1)} %collective-permute-done.2.ahead, ...), custom_call_target="tpu_custom_call" | custom-call | tf_op jit(solution)/shard_map/window/pallas_call | solution.py:295
  64.8 0.1 fusion.3
  65.0 4.6 %collective-permute-start.7 = (bf16[3,3,6,512]{3,2,1,0:T(8,128)(2,1)S(1)}, bf16[3,3,6,512]{3,2,1,0:T(8,128)(2,1)S(1)}, u32[]{:S(2)}, u32[]{:S(2)}) collective-permute-start(bf16[3,3,6,512]{3,2,1,0:T(8,128)(2,1)S(1)} %reshape.30), channel_id=1, source_target_pairs={{0,32},{1,481},{2,34},{3,483},{4,36},{5,485},{6,38},{7,487},{8,40}... | collective-permute-start | bytes 165896 | tf_op jit(solution)/shard_map/ppermute | solution.py:41
  69.6 6.3 %collective-permute-start.8 = (bf16[3,3,6,512]{3,2,1,0:T(8,128)(2,1)S(1)}, bf16[3,3,6,512]{3,2,1,0:T(8,128)(2,1)S(1)}, u32[]{:S(2)}, u32[]{:S(2)}) collective-permute-start(bf16[3,3,6,512]{3,2,1,0:T(8,128)(2,1)S(1)} %reshape.31), channel_id=1, source_target_pairs={{0,33},{1,482},{2,35},{3,484},{4,37},{5,486},{6,39},{7,488},{8,41}... | collective-permute-start | bytes 165896 | tf_op jit(solution)/shard_map/ppermute | solution.py:41
  75.9 1.9 %collective-permute-start.6 = (bf16[3,3,6,512]{3,2,1,0:T(8,128)(2,1)S(1)}, bf16[3,3,6,512]{3,2,1,0:T(8,128)(2,1)S(1)}, u32[]{:S(2)}, u32[]{:S(2)}) collective-permute-start(bf16[3,3,6,512]{3,2,1,0:T(8,128)(2,1)S(1)} %reshape.29), channel_id=1, source_target_pairs={{0,1},{1,2},{2,3},{3,4},{4,5},{5,6},{6,7},{7,8},{8,9},{9,10},{10,1... | collective-permute-start | bytes 165896 | tf_op jit(solution)/shard_map/ppermute | solution.py:41
  77.8 0.0 collective-permute-done.7
  77.8 1.6 %collective-permute-done.8 = bf16[3,3,6,512]{3,2,1,0:T(8,128)(2,1)S(1)} collective-permute-done((bf16[3,3,6,512]{3,2,1,0:T(8,128)(2,1)S(1)}, bf16[3,3,6,512]{3,2,1,0:T(8,128)(2,1)S(1)}, u32[]{:S(2)}, u32[]{:S(2)}) %collective-permute-start.8) | collective-permute-done | bytes 55328 | tf_op jit(solution)/shard_map/ppermute | solution.py:41
  79.5 0.0 collective-permute-done.6
  79.5 0.8 %maximum_select_fusion = bf16[3,6,12,512]{3,2,1,0:T(8,128)(2,1)} fusion(bf16[3,3,6,512]{3,2,1,0:T(8,128)(2,1)S(1)} %reshape.32, bf16[3,3,6,512]{3,2,1,0:T(8,128)(2,1)S(1)} %collective-permute-done.8, bf16[3,3,6,512]{3,2,1,0:T(8,128)(2,1)S(1)} %collective-permute-done.7, bf16[3,3,6,512]{3,2,1,0:T(8,128)(2,1)S(1)} %collective-permute-done.6, pred[]{:T(512)S(6)} %eq.11), kind=kLoop, calls=%fused_computation | loop fusion | flops 1880064 | bytes 442369 | tf_op jit(solution)/shard_map/jit(_where)/select_n | solution.py:327
  (6 shorter events, 0.1 us)
Async XLA Ops:
  0.8 14.0 %copy-start.4 = (bf16[13,6,12,512]{3,0,2,1:T(8,128)(2,1)S(1)}, bf16[13,6,12,512]{3,0,2,1:T(8,128)(2,1)}, u32[]{:S(2)}) copy-start(bf16[13,6,12,512]{3,0,2,1:T(8,128)(2,1)} %param.9) | copy-start | bytes 2875396
  1.8 40.4 %all-to-all-start = ((bf16[32,16,768]{2,1,0:T(8,128)(2,1)}), bf16[32,16,768]{2,1,0:T(8,128)(2,1)S(1)}, u32[]{:S(2)}, u32[]{:S(2)}) async-start(bf16[32,16,768]{2,1,0:T(8,128)(2,1)} %bitcast.5), calls=%async_computation | async-start | bytes 1572864 | tf_op jit(solution)/shard_map/all_to_all | solution.py:244
  14.8 0.7 copy-start.1
  15.4 42.6 %copy-start = (bf16[3,16,512]{2,1,0:T(8,128)(2,1)S(1)}, bf16[3,16,512]{2,1,0:T(8,128)(2,1)}, u32[]{:S(2)}) copy-start(bf16[3,16,512]{2,1,0:T(8,128)(2,1)} %param.10) | copy-start | bytes 147460
  15.5 44.8 %copy-start.2 = (bf16[3,512]{1,0:T(4,128)(2,1)S(1)}, bf16[3,512]{1,0:T(4,128)(2,1)}, u32[]{:S(2)}) copy-start(bf16[3,512]{1,0:T(4,128)(2,1)} %base.1) | copy-start | bytes 9220
  15.5 44.8 %copy-start.3 = (f32[512]{0:T(512)S(1)}, f32[512]{0:T(512)}, u32[]{:S(2)}) copy-start(f32[512]{0:T(512)} %param.14) | copy-start | bytes 6148
  18.4 19.1 %collective-permute-start = (bf16[240,512]{1,0:T(8,128)(2,1)S(1)}, bf16[240,512]{1,0:T(8,128)(2,1)S(1)}, u32[]{:S(2)}, u32[]{:S(2)}) collective-permute-start(bf16[240,512]{1,0:T(8,128)(2,1)S(1)} %get-tuple-element.21), channel_id=1, source_target_pairs={{32,0},{481,1},{34,2},{483,3},{36,4},{485,5},{38,6},{487,7},{40,8}... | collective-permute-start | bytes 737288 | tf_op jit(solution)/shard_map/ppermute | solution.py:36
  22.6 19.6 %collective-permute-start.1 = (bf16[240,512]{1,0:T(8,128)(2,1)S(1)}, bf16[240,512]{1,0:T(8,128)(2,1)S(1)}, u32[]{:S(2)}, u32[]{:S(2)}) collective-permute-start(bf16[240,512]{1,0:T(8,128)(2,1)S(1)} %get-tuple-element.22), channel_id=1, source_target_pairs={{33,0},{482,1},{35,2},{484,3},{37,4},{486,5},{39,6},{488,7},{41,8}... | collective-permute-start | bytes 737288 | tf_op jit(solution)/shard_map/ppermute | solution.py:36
  42.2 13.9 %collective-permute-start.2 = (bf16[512,768]{1,0:T(8,128)(2,1)S(1)}, bf16[512,768]{1,0:T(8,128)(2,1)S(1)}, u32[]{:S(2)}, u32[]{:S(2)}) collective-permute-start(bf16[512,768]{1,0:T(8,128)(2,1)S(1)} %bitcast.11), channel_id=1, source_target_pairs={{128,0},{385,1},{130,2},{387,3},{132,4},{389,5},{134,6},{391,7},{1... | collective-permute-start | bytes 2359304 | tf_op jit(solution)/shard_map/ppermute | solution.py:36
  44.1 7.8 %collective-permute-start.3 = (bf16[240,512]{1,0:T(8,128)(2,1)S(1)}, bf16[240,512]{1,0:T(8,128)(2,1)S(1)}, u32[]{:S(2)}, u32[]{:S(2)}) collective-permute-start(bf16[240,512]{1,0:T(8,128)(2,1)S(1)} %get-tuple-element.25), channel_id=1, source_target_pairs={{1,0},{2,1},{3,2},{4,3},{5,4},{6,5},{7,6},{8,7},{9,8},{10,9},{11,1... | collective-permute-start | bytes 737288 | tf_op jit(solution)/shard_map/ppermute | solution.py:36
  51.9 7.3 %collective-permute-start.4 = (bf16[512,768]{1,0:T(8,128)(2,1)S(1)}, bf16[512,768]{1,0:T(8,128)(2,1)S(1)}, u32[]{:S(2)}, u32[]{:S(2)}) collective-permute-start(bf16[512,768]{1,0:T(8,128)(2,1)S(1)} %bitcast.12), channel_id=1, source_target_pairs={{1,0},{0,1},{3,2},{2,3},{5,4},{4,5},{7,6},{6,7},{9,8},{8,9},{11,10... | collective-permute-start | bytes 2359304 | tf_op jit(solution)/shard_map/ppermute | solution.py:36
  56.1 4.2 %collective-permute-start.5 = (bf16[512,768]{1,0:T(8,128)(2,1)S(1)}, bf16[512,768]{1,0:T(8,128)(2,1)S(1)}, u32[]{:S(2)}, u32[]{:S(2)}) collective-permute-start(bf16[512,768]{1,0:T(8,128)(2,1)S(1)} %collective-permute-done.2.ahead), channel_id=1, source_target_pairs={{1,0},{0,1},{3,2},{2,3},{5,4},{4,5},{7,6},{6,7},{9,8},{8,9},{11,10... | collective-permute-start | bytes 2359304 | tf_op jit(solution)/shard_map/ppermute | solution.py:36
  65.0 12.9 %collective-permute-start.7 = (bf16[3,3,6,512]{3,2,1,0:T(8,128)(2,1)S(1)}, bf16[3,3,6,512]{3,2,1,0:T(8,128)(2,1)S(1)}, u32[]{:S(2)}, u32[]{:S(2)}) collective-permute-start(bf16[3,3,6,512]{3,2,1,0:T(8,128)(2,1)S(1)} %reshape.30), channel_id=1, source_target_pairs={{0,32},{1,481},{2,34},{3,483},{4,36},{5,485},{6,38},{7,487},{8,40}... | collective-permute-start | bytes 165896 | tf_op jit(solution)/shard_map/ppermute | solution.py:41
  69.6 9.9 %collective-permute-start.8 = (bf16[3,3,6,512]{3,2,1,0:T(8,128)(2,1)S(1)}, bf16[3,3,6,512]{3,2,1,0:T(8,128)(2,1)S(1)}, u32[]{:S(2)}, u32[]{:S(2)}) collective-permute-start(bf16[3,3,6,512]{3,2,1,0:T(8,128)(2,1)S(1)} %reshape.31), channel_id=1, source_target_pairs={{0,33},{1,482},{2,35},{3,484},{4,37},{5,486},{6,39},{7,488},{8,41}... | collective-permute-start | bytes 165896 | tf_op jit(solution)/shard_map/ppermute | solution.py:41
  75.9 3.6 %collective-permute-start.6 = (bf16[3,3,6,512]{3,2,1,0:T(8,128)(2,1)S(1)}, bf16[3,3,6,512]{3,2,1,0:T(8,128)(2,1)S(1)}, u32[]{:S(2)}, u32[]{:S(2)}) collective-permute-start(bf16[3,3,6,512]{3,2,1,0:T(8,128)(2,1)S(1)} %reshape.29), channel_id=1, source_target_pairs={{0,1},{1,2},{2,3},{3,4},{4,5},{5,6},{6,7},{7,8},{8,9},{9,10},{10,1... | collective-permute-start | bytes 165896 | tf_op jit(solution)/shard_map/ppermute | solution.py:41

commit v3 on v2

--- a/solution.py
+++ b/solution.py
@@ -65,14 +65,8 @@
     return i, j + 1 if j % 2 == 0 else j - 1
 
 
-def quarter_kernel(place, regions, far_tokens, own, east, band, corner, tokens, rows, arrived):
-    levels = tokens.shape[0]
-    copies = [
-        pltpu.make_async_copy(far_tokens.at[level], tokens.at[level], arrived.at[level])
-        for level in range(levels)
-    ]
-    for copy in copies:
-        copy.start()
+def quarter_kernel(place, regions, tokens, own, east, band, corner, rows):
+    levels = tokens.shape[2]
     odd = place[1]
     kept, sent = HALF_LAT * (1 - odd), HALF_LAT * odd
     for k in range(4):
@@ -80,26 +74,28 @@
         label = jnp.full((1, rows.shape[1]), label, jnp.int32)
         rows[levels * CELLS + k : levels * CELLS + k + 1] = label.astype(jnp.float32)
     rows[levels * CELLS + 4 :] = jnp.zeros((2, rows.shape[1]), jnp.float32)
-    for n, (out, top, left) in enumerate(
-        ((band, sent, HALF_LON), (corner, kept, 0), (east, sent, 0), (own, kept, HALF_LON))
+    for out, top, left in (
+        (band, sent, HALF_LON),
+        (corner, kept, 0),
+        (east, sent, 0),
+        (own, kept, HALF_LON),
     ):
-        for level in range(levels):
-            if n == 0:
-                copies[level].wait()
-            for r in range(HALF_LAT):
-                row = tokens[level, top + r].astype(jnp.float32)
-                at = level * CELLS + r * HALF_LON
-                rows[at : at + HALF_LON] = row[left : left + HALF_LON]
+        for r in range(HALF_LAT):
+            for c in range(HALF_LON):
+                at = (r * HALF_LON + c) * levels
+                rows[at : at + levels] = tokens[top + r, left + c].astype(jnp.float32)
         out[...] = rows[...].astype(out.dtype)
 
 
-def mix_kernel(levels, place, own, east, band, corner, probe, tokens, mix, labels, joined):
+def mix_kernel(levels, place, own, east, band, corner, probe, tokens, mix, labels, rows, joined):
     width = own.shape[1]
     cells = PADDED
     for k, part in enumerate((own, east, band, corner)):
-        rows = part[...].astype(jnp.float32)
-        for level in range(levels):
-            joined[level, k * CELLS : (k + 1) * CELLS] = rows[level * CELLS : (level + 1) * CELLS]
+        for t in range(rows.shape[0]):
+            rows[t] = part[:, t * 128 : (t + 1) * 128].astype(jnp.float32)
+            for level in range(levels):
+                at = pl.ds(level, CELLS, stride=levels)
+                joined[level, k * CELLS : (k + 1) * CELLS, t * 128 : (t + 1) * 128] = rows[t, at]
     joined[:, 4 * CELLS :] = jnp.zeros((levels, cells - 4 * CELLS, width), jnp.float32)
     x = joined[...].astype(jnp.bfloat16).reshape(levels * cells, width)
     tokens[...] = x
@@ -194,22 +190,26 @@
     pair = 2 * head_dim
     lane = lax.broadcasted_iota(jnp.int32, (1, pair), 1)
     left = jnp.where(lane < head_dim, 1.0, 0.0)
-    sides = (left.astype(bf16), (1.0 - left).astype(bf16))
+    scale = head_dim**-0.5
+    sides = ((left * scale).astype(bf16), ((1.0 - left) * scale).astype(bf16))
+    ones = jnp.ones((tokens_in, pair), bf16)
     attended = []
     for h in range(heads // 2):
         q = qkv[:, h * pair : (h + 1) * pair]
         k = qkv[:, width + h * pair : width + (h + 1) * pair]
         v = qkv[:, 2 * width + h * pair : 2 * width + (h + 1) * pair]
+        v = jnp.concatenate([v, ones], axis=1)
         both = []
         for side in sides:
             logits = lax.dot_general(
                 q * side, k, (((1,), (1,)), ((), ())), preferred_element_type=f32
             )
-            logits = jnp.where(allowed, logits / head_dim**0.5, -1e30)
-            grown = jnp.exp(logits - jnp.max(logits, axis=-1, keepdims=True))
-            grown = grown / jnp.sum(grown, axis=-1, keepdims=True)
-            both.append(jnp.dot(grown.astype(bf16), v, preferred_element_type=f32))
-        attended.append(jnp.where(lane < head_dim, both[0], both[1]).astype(bf16))
+            logits = jnp.where(allowed, logits, -1e30)
+            grown = jnp.exp(logits - jnp.max(logits, axis=-1, keepdims=True)).astype(bf16)
+            both.append(jnp.dot(grown, v, preferred_element_type=f32))
+        total = jnp.where(lane < head_dim, both[0][:, pair:], both[1][:, pair:])
+        sums = jnp.where(lane < head_dim, both[0][:, :pair], both[1][:, :pair])
+        attended.append((sums / total).astype(bf16))
     attended = jnp.concatenate(attended, axis=1)
     result = jnp.dot(attended, weights[:, 5 * width :], preferred_element_type=f32)
     result = (full + result.astype(bf16).astype(f32)).astype(bf16)
@@ -253,24 +253,19 @@
     own, east, band, corner = pl.pallas_call(
         quarter_kernel,
         out_shape=[quarter] * 4,
-        in_specs=[smem, smem, pl.BlockSpec(memory_space=pl.ANY)],
+        in_specs=[smem, smem, vmem],
         out_specs=[vmem] * 4,
-        scratch_shapes=[
-            pltpu.VMEM(level_tokens.shape, level_tokens.dtype),
-            pltpu.VMEM((packed, width), jnp.float32),
-            pltpu.SemaphoreType.DMA((levels,)),
-        ],
+        scratch_shapes=[pltpu.VMEM((packed, width), jnp.float32)],
         compiler_params=pltpu.CompilerParams(vmem_limit_bytes=LIMIT),
         name="quarters",
-    )(place, region_ids, level_tokens)
+    )(place, region_ids, jnp.transpose(level_tokens, (1, 2, 0, 3)))
     band = fetch(band, along)
     corner = fetch(corner, across)
     mine, band, corner, east = lax.optimization_barrier((mine, band, corner, east))
     ahead = fetch(mine, next_along_x)
     east = fetch(east, beside)
 
-    again, east = lax.optimization_barrier((mine, east))
-    mine_swapped = fetch(again, other_core)
+    mine_swapped = fetch(mine, other_core)
     ahead, east = lax.optimization_barrier((ahead, east))
     token_rows = levels * PADDED
     mixes = latents * pool_heads
@@ -283,7 +278,10 @@
         ],
         in_specs=[smem] + [vmem] * 5,
         out_specs=[vmem] * 3,
-        scratch_shapes=[pltpu.VMEM((levels, PADDED, width), jnp.float32)],
+        scratch_shapes=[
+            pltpu.VMEM((width // 128, packed, 128), jnp.float32),
+            pltpu.VMEM((levels, PADDED, width), jnp.float32),
+        ],
         compiler_params=pltpu.CompilerParams(vmem_limit_bytes=LIMIT),
         cost_estimate=pl.CostEstimate(
             flops=2 * token_rows * width * mixes, bytes_accessed=8 << 20, transcendentals=0

time: 80.8 us -> 80.1 us (level)
  Pallas kernels: 8.47 us -> 6.48 us
  starting transfers between devices: 44.8 us -> 46.6 us
    pallas_call x1, Pallas kernels: 2.78 us -> 0.86 us  [body(): pl.pallas_call(quarter_kernel, out_shape=[quarter] * 4, in_specs=[smem, s...]
    ppermute x6, starting transfers between devices: 19 us -> 20.6 us  [fetch(): return lax.ppermute(block, BOTH, route)]
  transfers between devices with their start and end apart: 10 -> 10, of which waited for: 6 -> 6; matrix products, arithmetic and copies ran while one was open for 1% -> 0% of each run, Pallas kernels for 5% -> 3%
where the time goes in v3:
time: 80.1 us; the launch traced here: 79.6 us
  starting transfers between devices  46.6 us (58%)
  waiting for transfers between devices  23.4 us (29%)
  Pallas kernels  6.48 us (8%)
  other arithmetic  1.72 us (2%)
  local copies, waits for them, and re-layouts  1.16 us (1%)
    ppermute x6, waiting for transfers between devices, fetch(): return lax.ppermute(block, BOTH, route)  22.1 us
    ppermute x6, starting transfers between devices, fetch(): return lax.ppermute(block, BOTH, route)  20.6 us
    all_to_all x1, starting transfers between devices, body(): mine = lax.all_to_all(mine, 'lon', 0, 0, tiled=True)  13.1 us
    ppermute x3, starting transfers between devices, give_back(): return lax.ppermute(block, BOTH, [(b, a) for a, b in route])  12.9 us
    pallas_call x1, Pallas kernels, body(): pl.pallas_call(functools.partial(window_kernel, HEADS, pool_heads), out_s...  4.14 us
  transfers between devices with their start and end apart: 10, of which 6 were waited for; matrix products, arithmetic and copies ran while one was open for 0% of the time, Pallas kernels for 3%

profile of v3, /device:TPU:1, one launch (start us, length us, event | category | flops | bytes accessed | tf_op | source)
XLA Modules:
  0.0 79.6 jit_solution(14589026620168504385)
XLA Ops:
  0.0 0.8 fusion.2
  0.8 0.0 copy-start
  0.8 0.0 copy-start.2
  0.9 1.0 %broadcast_in_dim.2 = bf16[16,2,16,768]{3,2,1,0:T(8,128)(2,1)} broadcast(bf16[2,16,768]{2,1,0:T(8,128)(2,1)S(1)} %pad_maximum_fusion), dimensions={1,2,3} | broadcast | bytes 835584 | tf_op jit(solution)/shard_map/broadcast_in_dim | solution.py:242
  1.8 0.0 copy-start.1
  1.8 13.1 %all-to-all-start = ((bf16[32,16,768]{2,1,0:T(8,128)(2,1)}), bf16[32,16,768]{2,1,0:T(8,128)(2,1)S(1)}, u32[]{:S(2)}, u32[]{:S(2)}) async-start(bf16[32,16,768]{2,1,0:T(8,128)(2,1)} %bitcast.6), calls=%async_computation | async-start | bytes 1572864 | tf_op jit(solution)/shard_map/all_to_all | solution.py:244
  14.9 0.0 copy-start.3
  15.0 0.0 copy-start.4
  15.0 0.1 pad_add_fusion.place
  15.1 0.0 copy-done
  15.1 0.0 copy-done.2
  15.1 0.9 %quarters.1 = (bf16[240,512]{1,0:T(8,128)(2,1)S(1)}, bf16[240,512]{1,0:T(8,128)(2,1)S(1)}, bf16[240,512]{1,0:T(8,128)(2,1)S(1)}, bf16[240,512]{1,0:T(8,128)(2,1)S(1)}) custom-call(s32[3]{0:T(128)S(1)} %pad_add_fusion.place, s32[6,12]{1,0:T(8,128)S(1)} %copy-done.2, bf16[6,12,13,512]{3,2,1,0:T(8,128)(2,1)S(1)} %bitcast.15), custom_call_target="tpu_custom_call" | custom-call | tf_op jit(solution)/shard_map/quarters/pallas_call | solution.py:253
  15.9 4.2 %collective-permute-start = (bf16[240,512]{1,0:T(8,128)(2,1)S(1)}, bf16[240,512]{1,0:T(8,128)(2,1)S(1)}, u32[]{:S(2)}, u32[]{:S(2)}) collective-permute-start(bf16[240,512]{1,0:T(8,128)(2,1)S(1)} %get-tuple-element.19), channel_id=1, source_target_pairs={{32,0},{481,1},{34,2},{483,3},{36,4},{485,5},{38,6},{487,7},{40,8}... | collective-permute-start | bytes 737288 | tf_op jit(solution)/shard_map/ppermute | solution.py:36
  20.2 7.1 %collective-permute-start.1 = (bf16[240,512]{1,0:T(8,128)(2,1)S(1)}, bf16[240,512]{1,0:T(8,128)(2,1)S(1)}, u32[]{:S(2)}, u32[]{:S(2)}) collective-permute-start(bf16[240,512]{1,0:T(8,128)(2,1)S(1)} %get-tuple-element.20), channel_id=1, source_target_pairs={{33,0},{482,1},{35,2},{484,3},{37,4},{486,5},{39,6},{488,7},{41,8}... | collective-permute-start | bytes 737288 | tf_op jit(solution)/shard_map/ppermute | solution.py:36
  27.3 11.8 %collective-permute-done.band = bf16[240,512]{1,0:T(8,128)(2,1)S(1)} collective-permute-done((bf16[240,512]{1,0:T(8,128)(2,1)S(1)}, bf16[240,512]{1,0:T(8,128)(2,1)S(1)}, u32[]{:S(2)}, u32[]{:S(2)}) %collective-permute-start) | collective-permute-done | bytes 245792 | tf_op jit(solution)/shard_map/ppermute | solution.py:36
  39.1 2.9 %collective-permute-done.1.corner = bf16[240,512]{1,0:T(8,128)(2,1)S(1)} collective-permute-done((bf16[240,512]{1,0:T(8,128)(2,1)S(1)}, bf16[240,512]{1,0:T(8,128)(2,1)S(1)}, u32[]{:S(2)}, u32[]{:S(2)}) %collective-permute-start.1) | collective-permute-done | bytes 245792 | tf_op jit(solution)/shard_map/ppermute | solution.py:36
  42.1 0.0 all-to-all-done
  42.1 1.9 %collective-permute-start.2 = (bf16[512,768]{1,0:T(8,128)(2,1)S(1)}, bf16[512,768]{1,0:T(8,128)(2,1)S(1)}, u32[]{:S(2)}, u32[]{:S(2)}) collective-permute-start(bf16[512,768]{1,0:T(8,128)(2,1)S(1)} %bitcast.12), channel_id=1, source_target_pairs={{128,0},{385,1},{130,2},{387,3},{132,4},{389,5},{134,6},{391,7},{1... | collective-permute-start | bytes 2359304 | tf_op jit(solution)/shard_map/ppermute | solution.py:36
  44.0 1.9 %collective-permute-start.3 = (bf16[240,512]{1,0:T(8,128)(2,1)S(1)}, bf16[240,512]{1,0:T(8,128)(2,1)S(1)}, u32[]{:S(2)}, u32[]{:S(2)}) collective-permute-start(bf16[240,512]{1,0:T(8,128)(2,1)S(1)} %get-tuple-element.23), channel_id=1, source_target_pairs={{1,0},{2,1},{3,2},{4,3},{5,4},{6,5},{7,6},{8,7},{9,8},{10,9},{11,1... | collective-permute-start | bytes 737288 | tf_op jit(solution)/shard_map/ppermute | solution.py:36
  45.9 3.5 %collective-permute-start.4 = (bf16[512,768]{1,0:T(8,128)(2,1)S(1)}, bf16[512,768]{1,0:T(8,128)(2,1)S(1)}, u32[]{:S(2)}, u32[]{:S(2)}) collective-permute-start(bf16[512,768]{1,0:T(8,128)(2,1)S(1)} %bitcast.13), channel_id=1, source_target_pairs={{1,0},{0,1},{3,2},{2,3},{5,4},{4,5},{7,6},{6,7},{9,8},{8,9},{11,10... | collective-permute-start | bytes 2359304 | tf_op jit(solution)/shard_map/ppermute | solution.py:36
  49.4 2.1 %collective-permute-done.3.east = bf16[240,512]{1,0:T(8,128)(2,1)S(1)} collective-permute-done((bf16[240,512]{1,0:T(8,128)(2,1)S(1)}, bf16[240,512]{1,0:T(8,128)(2,1)S(1)}, u32[]{:S(2)}, u32[]{:S(2)}) %collective-permute-start.3) | collective-permute-done | bytes 245792 | tf_op jit(solution)/shard_map/ppermute | solution.py:36
  51.5 4.5 %collective-permute-done.2.ahead = bf16[512,768]{1,0:T(8,128)(2,1)S(1)} collective-permute-done((bf16[512,768]{1,0:T(8,128)(2,1)S(1)}, bf16[512,768]{1,0:T(8,128)(2,1)S(1)}, u32[]{:S(2)}, u32[]{:S(2)}) %collective-permute-start.2) | collective-permute-done | bytes 786464 | tf_op jit(solution)/shard_map/ppermute | solution.py:36
  56.0 1.9 %collective-permute-start.5 = (bf16[512,768]{1,0:T(8,128)(2,1)S(1)}, bf16[512,768]{1,0:T(8,128)(2,1)S(1)}, u32[]{:S(2)}, u32[]{:S(2)}) collective-permute-start(bf16[512,768]{1,0:T(8,128)(2,1)S(1)} %collective-permute-done.2.ahead), channel_id=1, source_target_pairs={{1,0},{0,1},{3,2},{2,3},{5,4},{4,5},{7,6},{6,7},{9,8},{8,9},{11,10... | collective-permute-start | bytes 2359304 | tf_op jit(solution)/shard_map/ppermute | solution.py:36
  57.9 0.0 copy-done.1
  57.9 1.5 %mix.1 = (bf16[1040,512]{1,0:T(8,128)(2,1)S(1)}, bf16[1040,48]{1,0:T(8,128)(2,1)S(1)}, f32[8,128]{1,0:T(8,128)S(1)}) custom-call(s32[3]{0:T(128)S(1)} %pad_add_fusion.place, bf16[240,512]{1,0:T(8,128)(2,1)S(1)} %get-tuple-element.18.own, bf16[240,512]{1,0:T(8,128)(2,1)S(1)} %collective-permute-done.3.east, bf16[240,512]{1,0:T(8,128)(2,1)S(1)} %collective-permute-done.band, ...), custom_call_target="tpu_custom_call" | custom-call | flops 51118080 | bytes 8388608 | tf_op jit(solution)/shard_map/mix/pallas_call | solution.py:272
  59.4 0.0 collective-permute-done.4.mine_swapped
  59.4 0.7 collective-permute-done.5.ahead_swapped
  60.2 0.0 copy-done.3
  60.2 0.0 copy-done.4
  60.2 4.1 %window.1 = bf16[3,80,512]{2,1,0:T(8,128)(2,1)S(1)} custom-call(s32[3]{0:T(128)S(1)} %pad_add_fusion.place, bf16[1040,512]{1,0:T(8,128)(2,1)S(1)} %get-tuple-element.27.tokens, bf16[1040,48]{1,0:T(8,128)(2,1)S(1)} %get-tuple-element.28.mix, bf16[512,768]{1,0:T(8,128)(2,1)S(1)} %bitcast.14, bf16[512,768]{1,0:T(8,128)(2,1)S(1)} %collective-permute-done.2.ahead, ...), custom_call_target="tpu_custom_call" | custom-call | tf_op jit(solution)/shard_map/window/pallas_call | solution.py:293
  64.3 0.1 fusion.3
  64.5 2.6 %collective-permute-start.7 = (bf16[3,3,6,512]{3,2,1,0:T(8,128)(2,1)S(1)}, bf16[3,3,6,512]{3,2,1,0:T(8,128)(2,1)S(1)}, u32[]{:S(2)}, u32[]{:S(2)}) collective-permute-start(bf16[3,3,6,512]{3,2,1,0:T(8,128)(2,1)S(1)} %reshape.30), channel_id=1, source_target_pairs={{0,32},{1,481},{2,34},{3,483},{4,36},{5,485},{6,38},{7,487},{8,40}... | collective-permute-start | bytes 165896 | tf_op jit(solution)/shard_map/ppermute | solution.py:41
  67.1 8.4 %collective-permute-start.8 = (bf16[3,3,6,512]{3,2,1,0:T(8,128)(2,1)S(1)}, bf16[3,3,6,512]{3,2,1,0:T(8,128)(2,1)S(1)}, u32[]{:S(2)}, u32[]{:S(2)}) collective-permute-start(bf16[3,3,6,512]{3,2,1,0:T(8,128)(2,1)S(1)} %reshape.31), channel_id=1, source_target_pairs={{0,33},{1,482},{2,35},{3,484},{4,37},{5,486},{6,39},{7,488},{8,41}... | collective-permute-start | bytes 165896 | tf_op jit(solution)/shard_map/ppermute | solution.py:41
  75.5 1.9 %collective-permute-start.6 = (bf16[3,3,6,512]{3,2,1,0:T(8,128)(2,1)S(1)}, bf16[3,3,6,512]{3,2,1,0:T(8,128)(2,1)S(1)}, u32[]{:S(2)}, u32[]{:S(2)}) collective-permute-start(bf16[3,3,6,512]{3,2,1,0:T(8,128)(2,1)S(1)} %reshape.29), channel_id=1, source_target_pairs={{0,1},{1,2},{2,3},{3,4},{4,5},{5,6},{6,7},{7,8},{8,9},{9,10},{10,1... | collective-permute-start | bytes 165896 | tf_op jit(solution)/shard_map/ppermute | solution.py:41
  77.4 0.0 collective-permute-done.7
  77.5 0.0 collective-permute-done.8
  77.5 1.3 %collective-permute-done.6 = bf16[3,3,6,512]{3,2,1,0:T(8,128)(2,1)S(1)} collective-permute-done((bf16[3,3,6,512]{3,2,1,0:T(8,128)(2,1)S(1)}, bf16[3,3,6,512]{3,2,1,0:T(8,128)(2,1)S(1)}, u32[]{:S(2)}, u32[]{:S(2)}) %collective-permute-start.6) | collective-permute-done | bytes 55328 | tf_op jit(solution)/shard_map/ppermute | solution.py:41
  78.8 0.8 %maximum_select_fusion = bf16[3,6,12,512]{3,2,1,0:T(8,128)(2,1)} fusion(bf16[3,3,6,512]{3,2,1,0:T(8,128)(2,1)S(1)} %reshape.32, bf16[3,3,6,512]{3,2,1,0:T(8,128)(2,1)S(1)} %collective-permute-done.8, bf16[3,3,6,512]{3,2,1,0:T(8,128)(2,1)S(1)} %collective-permute-done.7, bf16[3,3,6,512]{3,2,1,0:T(8,128)(2,1)S(1)} %collective-permute-done.6, pred[]{:T(512)S(6)} %eq.11), kind=kLoop, calls=%fused_computation | loop fusion | flops 1880064 | bytes 442369 | tf_op jit(solution)/shard_map/jit(_where)/select_n | solution.py:325
  (6 shorter events, 0.1 us)
Async XLA Ops:
  0.8 14.3 %copy-start = (bf16[13,6,12,512]{3,0,2,1:T(8,128)(2,1)S(1)}, bf16[13,6,12,512]{3,0,2,1:T(8,128)(2,1)}, u32[]{:S(2)}) copy-start(bf16[13,6,12,512]{3,0,2,1:T(8,128)(2,1)} %param.9) | copy-start | bytes 2875396
  0.8 14.2 %copy-start.2 = (s32[6,12]{1,0:T(8,128)S(1)}, s32[6,12]{1,0:T(8,128)}, u32[]{:S(2)}) copy-start(s32[6,12]{1,0:T(8,128)} %regions.1) | copy-start | bytes 868
  1.8 56.1 %copy-start.1 = (bf16[3,16,512]{2,1,0:T(8,128)(2,1)S(1)}, bf16[3,16,512]{2,1,0:T(8,128)(2,1)}, u32[]{:S(2)}) copy-start(bf16[3,16,512]{2,1,0:T(8,128)(2,1)} %param.10) | copy-start | bytes 147460
  1.8 40.2 %all-to-all-start = ((bf16[32,16,768]{2,1,0:T(8,128)(2,1)}), bf16[32,16,768]{2,1,0:T(8,128)(2,1)S(1)}, u32[]{:S(2)}, u32[]{:S(2)}) async-start(bf16[32,16,768]{2,1,0:T(8,128)(2,1)} %bitcast.6), calls=%async_computation | async-start | bytes 1572864 | tf_op jit(solution)/shard_map/all_to_all | solution.py:244
  14.9 45.2 %copy-start.3 = (bf16[3,512]{1,0:T(4,128)(2,1)S(1)}, bf16[3,512]{1,0:T(4,128)(2,1)}, u32[]{:S(2)}) copy-start(bf16[3,512]{1,0:T(4,128)(2,1)} %base.1) | copy-start | bytes 9220
  15.0 45.2 %copy-start.4 = (f32[512]{0:T(512)S(1)}, f32[512]{0:T(512)}, u32[]{:S(2)}) copy-start(f32[512]{0:T(512)} %param.14) | copy-start | bytes 6148
  15.9 23.2 %collective-permute-start = (bf16[240,512]{1,0:T(8,128)(2,1)S(1)}, bf16[240,512]{1,0:T(8,128)(2,1)S(1)}, u32[]{:S(2)}, u32[]{:S(2)}) collective-permute-start(bf16[240,512]{1,0:T(8,128)(2,1)S(1)} %get-tuple-element.19), channel_id=1, source_target_pairs={{32,0},{481,1},{34,2},{483,3},{36,4},{485,5},{38,6},{487,7},{40,8}... | collective-permute-start | bytes 737288 | tf_op jit(solution)/shard_map/ppermute | solution.py:36
  20.2 21.9 %collective-permute-start.1 = (bf16[240,512]{1,0:T(8,128)(2,1)S(1)}, bf16[240,512]{1,0:T(8,128)(2,1)S(1)}, u32[]{:S(2)}, u32[]{:S(2)}) collective-permute-start(bf16[240,512]{1,0:T(8,128)(2,1)S(1)} %get-tuple-element.20), channel_id=1, source_target_pairs={{33,0},{482,1},{35,2},{484,3},{37,4},{486,5},{39,6},{488,7},{41,8}... | collective-permute-start | bytes 737288 | tf_op jit(solution)/shard_map/ppermute | solution.py:36
  42.1 13.9 %collective-permute-start.2 = (bf16[512,768]{1,0:T(8,128)(2,1)S(1)}, bf16[512,768]{1,0:T(8,128)(2,1)S(1)}, u32[]{:S(2)}, u32[]{:S(2)}) collective-permute-start(bf16[512,768]{1,0:T(8,128)(2,1)S(1)} %bitcast.12), channel_id=1, source_target_pairs={{128,0},{385,1},{130,2},{387,3},{132,4},{389,5},{134,6},{391,7},{1... | collective-permute-start | bytes 2359304 | tf_op jit(solution)/shard_map/ppermute | solution.py:36
  44.0 7.5 %collective-permute-start.3 = (bf16[240,512]{1,0:T(8,128)(2,1)S(1)}, bf16[240,512]{1,0:T(8,128)(2,1)S(1)}, u32[]{:S(2)}, u32[]{:S(2)}) collective-permute-start(bf16[240,512]{1,0:T(8,128)(2,1)S(1)} %get-tuple-element.23), channel_id=1, source_target_pairs={{1,0},{2,1},{3,2},{4,3},{5,4},{6,5},{7,6},{8,7},{9,8},{10,9},{11,1... | collective-permute-start | bytes 737288 | tf_op jit(solution)/shard_map/ppermute | solution.py:36
  45.9 13.5 %collective-permute-start.4 = (bf16[512,768]{1,0:T(8,128)(2,1)S(1)}, bf16[512,768]{1,0:T(8,128)(2,1)S(1)}, u32[]{:S(2)}, u32[]{:S(2)}) collective-permute-start(bf16[512,768]{1,0:T(8,128)(2,1)S(1)} %bitcast.13), channel_id=1, source_target_pairs={{1,0},{0,1},{3,2},{2,3},{5,4},{4,5},{7,6},{6,7},{9,8},{8,9},{11,10... | collective-permute-start | bytes 2359304 | tf_op jit(solution)/shard_map/ppermute | solution.py:36
  56.0 4.2 %collective-permute-start.5 = (bf16[512,768]{1,0:T(8,128)(2,1)S(1)}, bf16[512,768]{1,0:T(8,128)(2,1)S(1)}, u32[]{:S(2)}, u32[]{:S(2)}) collective-permute-start(bf16[512,768]{1,0:T(8,128)(2,1)S(1)} %collective-permute-done.2.ahead), channel_id=1, source_target_pairs={{1,0},{0,1},{3,2},{2,3},{5,4},{4,5},{7,6},{6,7},{9,8},{8,9},{11,10... | collective-permute-start | bytes 2359304 | tf_op jit(solution)/shard_map/ppermute | solution.py:36
  64.5 13.0 %collective-permute-start.7 = (bf16[3,3,6,512]{3,2,1,0:T(8,128)(2,1)S(1)}, bf16[3,3,6,512]{3,2,1,0:T(8,128)(2,1)S(1)}, u32[]{:S(2)}, u32[]{:S(2)}) collective-permute-start(bf16[3,3,6,512]{3,2,1,0:T(8,128)(2,1)S(1)} %reshape.30), channel_id=1, source_target_pairs={{0,32},{1,481},{2,34},{3,483},{4,36},{5,485},{6,38},{7,487},{8,40}... | collective-permute-start | bytes 165896 | tf_op jit(solution)/shard_map/ppermute | solution.py:41
  67.1 10.4 %collective-permute-start.8 = (bf16[3,3,6,512]{3,2,1,0:T(8,128)(2,1)S(1)}, bf16[3,3,6,512]{3,2,1,0:T(8,128)(2,1)S(1)}, u32[]{:S(2)}, u32[]{:S(2)}) collective-permute-start(bf16[3,3,6,512]{3,2,1,0:T(8,128)(2,1)S(1)} %reshape.31), channel_id=1, source_target_pairs={{0,33},{1,482},{2,35},{3,484},{4,37},{5,486},{6,39},{7,488},{8,41}... | collective-permute-start | bytes 165896 | tf_op jit(solution)/shard_map/ppermute | solution.py:41
  75.5 3.3 %collective-permute-start.6 = (bf16[3,3,6,512]{3,2,1,0:T(8,128)(2,1)S(1)}, bf16[3,3,6,512]{3,2,1,0:T(8,128)(2,1)S(1)}, u32[]{:S(2)}, u32[]{:S(2)}) collective-permute-start(bf16[3,3,6,512]{3,2,1,0:T(8,128)(2,1)S(1)} %reshape.29), channel_id=1, source_target_pairs={{0,1},{1,2},{2,3},{3,4},{4,5},{5,6},{6,7},{7,8},{8,9},{9,10},{10,1... | collective-permute-start | bytes 165896 | tf_op jit(solution)/shard_map/ppermute | solution.py:41

commit v4 on v3

--- a/solution.py
+++ b/solution.py
@@ -139,7 +139,7 @@
     latents, width = base.shape
     cells = PADDED
     level_count = tokens.shape[0] // cells
-    columns = mine.shape[1]
+    columns = mine.shape[2]
     f32 = jnp.float32
     bf16 = jnp.bfloat16
     parity, core = place[0], place[1]
@@ -149,10 +149,13 @@
         (mine_swapped, parity, 1 - core),
         (ahead_swapped, 1 - parity, 1 - core),
     ):
-        start = (group * 2 + side) * columns
-        weights[:, pl.ds(pl.multiple_of(start, 128), columns)] = ref[...]
-
-    values[...] = jnp.dot(tokens[...], weights[:, :width], preferred_element_type=f32)
+        start = pl.ds(pl.multiple_of(group * columns, 128), columns)
+        weights[:, side, :, start] = ref[...]
+
+    def weight(first, last):
+        return weights[:, :, :, first:last].reshape(width, last - first)
+
+    values[...] = jnp.dot(tokens[...], weight(0, width), preferred_element_type=f32)
     span = width // pool_heads
     head_of = lax.broadcasted_iota(jnp.int32, (latents * pool_heads, width), 1) // span
     row_of = lax.broadcasted_iota(jnp.int32, (latents * pool_heads, width), 0)
@@ -162,7 +165,7 @@
         share = jnp.dot(mix[...], spread, preferred_element_type=f32) * values[...]
         pooled.append(jnp.sum(share.reshape(level_count, cells, width), axis=0).astype(bf16))
     pooled = jnp.concatenate(pooled, axis=0)
-    latent = jnp.dot(pooled, weights[:, width : 2 * width], preferred_element_type=f32)
+    latent = jnp.dot(pooled, weight(width, 2 * width), preferred_element_type=f32)
     base_rows = jnp.broadcast_to(base[...].astype(f32)[:, None, :], (latents, cells, width))
     latent = (latent + base_rows.reshape(latents * cells, width)).astype(bf16)
 
@@ -170,7 +173,7 @@
     centred = full - jnp.mean(full, axis=-1, keepdims=True)
     variance = jnp.mean(centred * centred, axis=-1, keepdims=True)
     normed = (centred * lax.rsqrt(variance + STABILIZER_TINY) * gain[...]).astype(bf16)
-    qkv = jnp.dot(normed, weights[:, 2 * width : 5 * width], preferred_element_type=f32)
+    qkv = jnp.dot(normed, weight(2 * width, 5 * width), preferred_element_type=f32)
     qkv = qkv.astype(bf16)
 
     tokens_in = latents * cells
@@ -211,7 +214,7 @@
         sums = jnp.where(lane < head_dim, both[0][:, :pair], both[1][:, :pair])
         attended.append((sums / total).astype(bf16))
     attended = jnp.concatenate(attended, axis=1)
-    result = jnp.dot(attended, weights[:, 5 * width :], preferred_element_type=f32)
+    result = jnp.dot(attended, weight(5 * width, 6 * width), preferred_element_type=f32)
     result = (full + result.astype(bf16).astype(f32)).astype(bf16)
     out[...] = result.reshape(latents, cells, width)
 
@@ -236,13 +239,12 @@
 
     joined = jnp.concatenate([value_weight, pool_out_weight, qkv_weight, attn_out_weight], axis=1)
     piece_rows, all_columns = joined.shape
-    columns = all_columns // 4
-    both = lax.dynamic_slice(joined, (0, parity * 2 * columns), (piece_rows, 2 * columns))
-    mine = jnp.stack([both[:, :columns], both[:, columns:]])
-    mine = jnp.broadcast_to(mine[None], (lon_count // 2, 2, piece_rows, columns))
-    mine = mine.reshape(lon_count, piece_rows, columns)
-    mine = lax.all_to_all(mine, "lon", 0, 0, tiled=True)
-    mine = mine.reshape(lon_count * piece_rows, columns)
+    half = all_columns // 2
+    groups = lon_count // 2
+    mine = lax.dynamic_slice(joined, (0, parity * half), (piece_rows, half))
+    mine = jnp.broadcast_to(mine[None], (groups, piece_rows, half))
+    same_core = [list(range(core, lon_count, 2)) for core in range(2)]
+    mine = lax.all_to_all(mine, "lon", 0, 0, tiled=True, axis_index_groups=same_core)
 
     vmem = pl.BlockSpec(memory_space=pltpu.VMEM)
     smem = pl.BlockSpec(memory_space=pltpu.SMEM)
@@ -296,7 +298,7 @@
         in_specs=[smem] + [vmem] * 9,
         out_specs=vmem,
         scratch_shapes=[
-            pltpu.VMEM((width, all_columns), jnp.bfloat16),
+            pltpu.VMEM((groups, 2, piece_rows, all_columns), jnp.bfloat16),
             pltpu.VMEM((token_rows, width), jnp.float32),
         ],
         compiler_params=pltpu.CompilerParams(vmem_limit_bytes=LIMIT),

time: 80.1 us -> 79.9 us (level)
  starting transfers between devices: 46.6 us -> 45.5 us
  waiting for transfers between devices: 23.4 us -> 24.3 us
    all_to_all x1, starting transfers between devices: 13.1 us -> 12.1 us  [body(): lax.all_to_all(mine, 'lon', 0, 0, tiled=True, axis_index_groups=same_core)]
    ppermute x6, waiting for transfers between devices: 22.1 us -> 23 us  [fetch(): return lax.ppermute(block, BOTH, route)]
  transfers between devices with their start and end apart: 10 -> 10, of which waited for: 6 -> 7; matrix products, arithmetic and copies ran while one was open for 0% -> 0% of each run, Pallas kernels for 3% -> 3%
where the time goes in v4:
time: 79.9 us; the launch traced here: 79.4 us
  starting transfers between devices  45.5 us (57%)
  waiting for transfers between devices  24.3 us (30%)
  Pallas kernels  6.47 us (8%)
  other arithmetic  1.71 us (2%)
  local copies, waits for them, and re-layouts  1.16 us (1%)
    ppermute x6, waiting for transfers between devices, fetch(): return lax.ppermute(block, BOTH, route)  23 us
    ppermute x6, starting transfers between devices, fetch(): return lax.ppermute(block, BOTH, route)  20.7 us
    ppermute x3, starting transfers between devices, give_back(): return lax.ppermute(block, BOTH, [(b, a) for a, b in route])  12.8 us
    all_to_all x1, starting transfers between devices, body(): lax.all_to_all(mine, 'lon', 0, 0, tiled=True, axis_index_groups=same_core)  12.1 us
    pallas_call x1, Pallas kernels, body(): pl.pallas_call(functools.partial(window_kernel, HEADS, pool_heads), out_s...  4.13 us
  transfers between devices with their start and end apart: 10, of which 7 were waited for; matrix products, arithmetic and copies ran while one was open for 0% of the time, Pallas kernels for 3%

profile of v4, /device:TPU:1, one launch (start us, length us, event | category | flops | bytes accessed | tf_op | source)
XLA Modules:
  0.0 79.4 jit_solution(569434618808141255)
XLA Ops:
  0.0 0.8 fusion.2
  0.8 0.0 copy-start
  0.8 0.0 copy-start.2
  0.8 1.0 %broadcast_in_dim.2 = bf16[16,16,1536]{2,1,0:T(8,128)(2,1)} broadcast(bf16[16,1536]{1,0:T(8,128)(2,1)S(1)} %fusion.2), dimensions={1,2} | broadcast | bytes 835584 | tf_op jit(solution)/shard_map/broadcast_in_dim | solution.py:245
  1.8 0.0 copy-start.1
  1.8 12.1 %all-to-all-start = ((bf16[16,16,1536]{2,1,0:T(8,128)(2,1)}), bf16[16,16,1536]{2,1,0:T(8,128)(2,1)S(1)}, u32[]{:S(2)}, u32[]{:S(2)}) async-start(bf16[16,16,1536]{2,1,0:T(8,128)(2,1)} %broadcast_in_dim.2), calls=%async_computation | async-start | bytes 1572864 | tf_op jit(solution)/shard_map/all_to_all | solution.py:247
  13.9 0.0 copy-start.3
  13.9 0.0 copy-start.4
  14.0 0.1 pad_add_fusion.place
  14.0 0.0 copy-done
  14.0 0.0 copy-done.2
  14.1 0.9 %quarters.1 = (bf16[240,512]{1,0:T(8,128)(2,1)S(1)}, bf16[240,512]{1,0:T(8,128)(2,1)S(1)}, bf16[240,512]{1,0:T(8,128)(2,1)S(1)}, bf16[240,512]{1,0:T(8,128)(2,1)S(1)}) custom-call(s32[3]{0:T(128)S(1)} %pad_add_fusion.place, s32[6,12]{1,0:T(8,128)S(1)} %copy-done.2, bf16[6,12,13,512]{3,2,1,0:T(8,128)(2,1)S(1)} %bitcast.6), custom_call_target="tpu_custom_call" | custom-call | tf_op jit(solution)/shard_map/quarters/pallas_call | solution.py:255
  14.9 4.2 %collective-permute-start = (bf16[240,512]{1,0:T(8,128)(2,1)S(1)}, bf16[240,512]{1,0:T(8,128)(2,1)S(1)}, u32[]{:S(2)}, u32[]{:S(2)}) collective-permute-start(bf16[240,512]{1,0:T(8,128)(2,1)S(1)} %get-tuple-element.19), channel_id=1, source_target_pairs={{32,0},{481,1},{34,2},{483,3},{36,4},{485,5},{38,6},{487,7},{40,8}... | collective-permute-start | bytes 737288 | tf_op jit(solution)/shard_map/ppermute | solution.py:36
  19.1 7.9 %collective-permute-start.1 = (bf16[240,512]{1,0:T(8,128)(2,1)S(1)}, bf16[240,512]{1,0:T(8,128)(2,1)S(1)}, u32[]{:S(2)}, u32[]{:S(2)}) collective-permute-start(bf16[240,512]{1,0:T(8,128)(2,1)S(1)} %get-tuple-element.20), channel_id=1, source_target_pairs={{33,0},{482,1},{35,2},{484,3},{37,4},{486,5},{39,6},{488,7},{41,8}... | collective-permute-start | bytes 737288 | tf_op jit(solution)/shard_map/ppermute | solution.py:36
  27.0 9.4 %collective-permute-done.band = bf16[240,512]{1,0:T(8,128)(2,1)S(1)} collective-permute-done((bf16[240,512]{1,0:T(8,128)(2,1)S(1)}, bf16[240,512]{1,0:T(8,128)(2,1)S(1)}, u32[]{:S(2)}, u32[]{:S(2)}) %collective-permute-start) | collective-permute-done | bytes 245792 | tf_op jit(solution)/shard_map/ppermute | solution.py:36
  36.4 5.6 %collective-permute-done.1.corner = bf16[240,512]{1,0:T(8,128)(2,1)S(1)} collective-permute-done((bf16[240,512]{1,0:T(8,128)(2,1)S(1)}, bf16[240,512]{1,0:T(8,128)(2,1)S(1)}, u32[]{:S(2)}, u32[]{:S(2)}) %collective-permute-start.1) | collective-permute-done | bytes 245792 | tf_op jit(solution)/shard_map/ppermute | solution.py:36
  42.0 0.0 all-to-all-done.mine
  42.0 1.9 %collective-permute-start.2 = (bf16[16,16,1536]{2,1,0:T(8,128)(2,1)S(1)}, bf16[16,16,1536]{2,1,0:T(8,128)(2,1)S(1)}, u32[]{:S(2)}, u32[]{:S(2)}) collective-permute-start(bf16[16,16,1536]{2,1,0:T(8,128)(2,1)S(1)} %all-to-all-done.mine), channel_id=1, source_target_pairs={{128,0},{385,1},{130,2},{387,3},{132,4},{389,5},{134,6},{391,7},{1... | collective-permute-start | bytes 2359304 | tf_op jit(solution)/shard_map/ppermute | solution.py:36
  43.9 1.9 %collective-permute-start.3 = (bf16[240,512]{1,0:T(8,128)(2,1)S(1)}, bf16[240,512]{1,0:T(8,128)(2,1)S(1)}, u32[]{:S(2)}, u32[]{:S(2)}) collective-permute-start(bf16[240,512]{1,0:T(8,128)(2,1)S(1)} %get-tuple-element.23), channel_id=1, source_target_pairs={{1,0},{2,1},{3,2},{4,3},{5,4},{6,5},{7,6},{8,7},{9,8},{10,9},{11,1... | collective-permute-start | bytes 737288 | tf_op jit(solution)/shard_map/ppermute | solution.py:36
  45.8 2.8 %collective-permute-start.4 = (bf16[16,16,1536]{2,1,0:T(8,128)(2,1)S(1)}, bf16[16,16,1536]{2,1,0:T(8,128)(2,1)S(1)}, u32[]{:S(2)}, u32[]{:S(2)}) collective-permute-start(bf16[16,16,1536]{2,1,0:T(8,128)(2,1)S(1)} %all-to-all-done.mine), channel_id=1, source_target_pairs={{1,0},{0,1},{3,2},{2,3},{5,4},{4,5},{7,6},{6,7},{9,8},{8,9},{11,10... | collective-permute-start | bytes 2359304 | tf_op jit(solution)/shard_map/ppermute | solution.py:36
  48.7 2.7 %collective-permute-done.3.east = bf16[240,512]{1,0:T(8,128)(2,1)S(1)} collective-permute-done((bf16[240,512]{1,0:T(8,128)(2,1)S(1)}, bf16[240,512]{1,0:T(8,128)(2,1)S(1)}, u32[]{:S(2)}, u32[]{:S(2)}) %collective-permute-start.3) | collective-permute-done | bytes 245792 | tf_op jit(solution)/shard_map/ppermute | solution.py:36
  51.4 4.5 %collective-permute-done.2.ahead = bf16[16,16,1536]{2,1,0:T(8,128)(2,1)S(1)} collective-permute-done((bf16[16,16,1536]{2,1,0:T(8,128)(2,1)S(1)}, bf16[16,16,1536]{2,1,0:T(8,128)(2,1)S(1)}, u32[]{:S(2)}, u32[]{:S(2)}) %collective-permute-start.2) | collective-permute-done | bytes 786464 | tf_op jit(solution)/shard_map/ppermute | solution.py:36
  55.9 1.9 %collective-permute-start.5 = (bf16[16,16,1536]{2,1,0:T(8,128)(2,1)S(1)}, bf16[16,16,1536]{2,1,0:T(8,128)(2,1)S(1)}, u32[]{:S(2)}, u32[]{:S(2)}) collective-permute-start(bf16[16,16,1536]{2,1,0:T(8,128)(2,1)S(1)} %collective-permute-done.2.ahead), channel_id=1, source_target_pairs={{1,0},{0,1},{3,2},{2,3},{5,4},{4,5},{7,6},{6,7},{9,8},{8,9},{11,10... | collective-permute-start | bytes 2359304 | tf_op jit(solution)/shard_map/ppermute | solution.py:36
  57.9 0.0 copy-done.1
  57.9 1.5 %mix.1 = (bf16[1040,512]{1,0:T(8,128)(2,1)S(1)}, bf16[1040,48]{1,0:T(8,128)(2,1)S(1)}, f32[8,128]{1,0:T(8,128)S(1)}) custom-call(s32[3]{0:T(128)S(1)} %pad_add_fusion.place, bf16[240,512]{1,0:T(8,128)(2,1)S(1)} %get-tuple-element.18.own, bf16[240,512]{1,0:T(8,128)(2,1)S(1)} %collective-permute-done.3.east, bf16[240,512]{1,0:T(8,128)(2,1)S(1)} %collective-permute-done.band, ...), custom_call_target="tpu_custom_call" | custom-call | flops 51118080 | bytes 8388608 | tf_op jit(solution)/shard_map/mix/pallas_call | solution.py:274
  59.4 0.0 collective-permute-done.4.mine_swapped
  59.4 0.7 collective-permute-done.5.ahead_swapped
  60.1 0.0 copy-done.3
  60.1 0.0 copy-done.4
  60.1 4.1 %window.1 = bf16[3,80,512]{2,1,0:T(8,128)(2,1)S(1)} custom-call(s32[3]{0:T(128)S(1)} %pad_add_fusion.place, bf16[1040,512]{1,0:T(8,128)(2,1)S(1)} %get-tuple-element.27.tokens, bf16[1040,48]{1,0:T(8,128)(2,1)S(1)} %get-tuple-element.28.mix, bf16[16,16,1536]{2,1,0:T(8,128)(2,1)S(1)} %all-to-all-done.mine, ...), custom_call_target="tpu_custom_call" | custom-call | tf_op jit(solution)/shard_map/window/pallas_call | solution.py:295
  64.2 0.1 fusion.3
  64.4 3.9 %collective-permute-start.7 = (bf16[3,3,6,512]{3,2,1,0:T(8,128)(2,1)S(1)}, bf16[3,3,6,512]{3,2,1,0:T(8,128)(2,1)S(1)}, u32[]{:S(2)}, u32[]{:S(2)}) collective-permute-start(bf16[3,3,6,512]{3,2,1,0:T(8,128)(2,1)S(1)} %reshape.22), channel_id=1, source_target_pairs={{0,32},{1,481},{2,34},{3,483},{4,36},{5,485},{6,38},{7,487},{8,40}... | collective-permute-start | bytes 165896 | tf_op jit(solution)/shard_map/ppermute | solution.py:41
  68.3 6.9 %collective-permute-start.8 = (bf16[3,3,6,512]{3,2,1,0:T(8,128)(2,1)S(1)}, bf16[3,3,6,512]{3,2,1,0:T(8,128)(2,1)S(1)}, u32[]{:S(2)}, u32[]{:S(2)}) collective-permute-start(bf16[3,3,6,512]{3,2,1,0:T(8,128)(2,1)S(1)} %reshape.23), channel_id=1, source_target_pairs={{0,33},{1,482},{2,35},{3,484},{4,37},{5,486},{6,39},{7,488},{8,41}... | collective-permute-start | bytes 165896 | tf_op jit(solution)/shard_map/ppermute | solution.py:41
  75.3 1.9 %collective-permute-start.6 = (bf16[3,3,6,512]{3,2,1,0:T(8,128)(2,1)S(1)}, bf16[3,3,6,512]{3,2,1,0:T(8,128)(2,1)S(1)}, u32[]{:S(2)}, u32[]{:S(2)}) collective-permute-start(bf16[3,3,6,512]{3,2,1,0:T(8,128)(2,1)S(1)} %reshape.21), channel_id=1, source_target_pairs={{0,1},{1,2},{2,3},{3,4},{4,5},{5,6},{6,7},{7,8},{8,9},{9,10},{10,1... | collective-permute-start | bytes 165896 | tf_op jit(solution)/shard_map/ppermute | solution.py:41
  77.2 0.0 collective-permute-done.7
  77.2 1.0 %collective-permute-done.8 = bf16[3,3,6,512]{3,2,1,0:T(8,128)(2,1)S(1)} collective-permute-done((bf16[3,3,6,512]{3,2,1,0:T(8,128)(2,1)S(1)}, bf16[3,3,6,512]{3,2,1,0:T(8,128)(2,1)S(1)}, u32[]{:S(2)}, u32[]{:S(2)}) %collective-permute-start.8) | collective-permute-done | bytes 55328 | tf_op jit(solution)/shard_map/ppermute | solution.py:41
  78.2 0.4 collective-permute-done.6
  78.6 0.8 %maximum_select_fusion = bf16[3,6,12,512]{3,2,1,0:T(8,128)(2,1)} fusion(bf16[3,3,6,512]{3,2,1,0:T(8,128)(2,1)S(1)} %reshape.24, bf16[3,3,6,512]{3,2,1,0:T(8,128)(2,1)S(1)} %collective-permute-done.8, bf16[3,3,6,512]{3,2,1,0:T(8,128)(2,1)S(1)} %collective-permute-done.7, bf16[3,3,6,512]{3,2,1,0:T(8,128)(2,1)S(1)} %collective-permute-done.6, pred[]{:T(512)S(6)} %eq.11), kind=kLoop, calls=%fused_computation | loop fusion | flops 1880064 | bytes 442369 | tf_op jit(solution)/shard_map/jit(_where)/select_n | solution.py:327
  (4 shorter events, 0.1 us)
Async XLA Ops:
  0.8 13.2 %copy-start = (bf16[13,6,12,512]{3,0,2,1:T(8,128)(2,1)S(1)}, bf16[13,6,12,512]{3,0,2,1:T(8,128)(2,1)}, u32[]{:S(2)}) copy-start(bf16[13,6,12,512]{3,0,2,1:T(8,128)(2,1)} %param.9) | copy-start | bytes 2875396
  0.8 13.2 %copy-start.2 = (s32[6,12]{1,0:T(8,128)S(1)}, s32[6,12]{1,0:T(8,128)}, u32[]{:S(2)}) copy-start(s32[6,12]{1,0:T(8,128)} %regions.1) | copy-start | bytes 868
  1.8 56.1 %copy-start.1 = (bf16[3,16,512]{2,1,0:T(8,128)(2,1)S(1)}, bf16[3,16,512]{2,1,0:T(8,128)(2,1)}, u32[]{:S(2)}) copy-start(bf16[3,16,512]{2,1,0:T(8,128)(2,1)} %param.10) | copy-start | bytes 147460
  1.8 40.2 %all-to-all-start = ((bf16[16,16,1536]{2,1,0:T(8,128)(2,1)}), bf16[16,16,1536]{2,1,0:T(8,128)(2,1)S(1)}, u32[]{:S(2)}, u32[]{:S(2)}) async-start(bf16[16,16,1536]{2,1,0:T(8,128)(2,1)} %broadcast_in_dim.2), calls=%async_computation | async-start | bytes 1572864 | tf_op jit(solution)/shard_map/all_to_all | solution.py:247
  13.9 46.2 %copy-start.3 = (bf16[3,512]{1,0:T(4,128)(2,1)S(1)}, bf16[3,512]{1,0:T(4,128)(2,1)}, u32[]{:S(2)}) copy-start(bf16[3,512]{1,0:T(4,128)(2,1)} %base.1) | copy-start | bytes 9220
  13.9 46.2 %copy-start.4 = (f32[512]{0:T(512)S(1)}, f32[512]{0:T(512)}, u32[]{:S(2)}) copy-start(f32[512]{0:T(512)} %param.14) | copy-start | bytes 6148
  14.9 21.5 %collective-permute-start = (bf16[240,512]{1,0:T(8,128)(2,1)S(1)}, bf16[240,512]{1,0:T(8,128)(2,1)S(1)}, u32[]{:S(2)}, u32[]{:S(2)}) collective-permute-start(bf16[240,512]{1,0:T(8,128)(2,1)S(1)} %get-tuple-element.19), channel_id=1, source_target_pairs={{32,0},{481,1},{34,2},{483,3},{36,4},{485,5},{38,6},{487,7},{40,8}... | collective-permute-start | bytes 737288 | tf_op jit(solution)/shard_map/ppermute | solution.py:36
  19.1 22.9 %collective-permute-start.1 = (bf16[240,512]{1,0:T(8,128)(2,1)S(1)}, bf16[240,512]{1,0:T(8,128)(2,1)S(1)}, u32[]{:S(2)}, u32[]{:S(2)}) collective-permute-start(bf16[240,512]{1,0:T(8,128)(2,1)S(1)} %get-tuple-element.20), channel_id=1, source_target_pairs={{33,0},{482,1},{35,2},{484,3},{37,4},{486,5},{39,6},{488,7},{41,8}... | collective-permute-start | bytes 737288 | tf_op jit(solution)/shard_map/ppermute | solution.py:36
  42.0 13.9 %collective-permute-start.2 = (bf16[16,16,1536]{2,1,0:T(8,128)(2,1)S(1)}, bf16[16,16,1536]{2,1,0:T(8,128)(2,1)S(1)}, u32[]{:S(2)}, u32[]{:S(2)}) collective-permute-start(bf16[16,16,1536]{2,1,0:T(8,128)(2,1)S(1)} %all-to-all-done.mine), channel_id=1, source_target_pairs={{128,0},{385,1},{130,2},{387,3},{132,4},{389,5},{134,6},{391,7},{1... | collective-permute-start | bytes 2359304 | tf_op jit(solution)/shard_map/ppermute | solution.py:36
  43.9 7.5 %collective-permute-start.3 = (bf16[240,512]{1,0:T(8,128)(2,1)S(1)}, bf16[240,512]{1,0:T(8,128)(2,1)S(1)}, u32[]{:S(2)}, u32[]{:S(2)}) collective-permute-start(bf16[240,512]{1,0:T(8,128)(2,1)S(1)} %get-tuple-element.23), channel_id=1, source_target_pairs={{1,0},{2,1},{3,2},{4,3},{5,4},{6,5},{7,6},{8,7},{9,8},{10,9},{11,1... | collective-permute-start | bytes 737288 | tf_op jit(solution)/shard_map/ppermute | solution.py:36
  45.8 13.5 %collective-permute-start.4 = (bf16[16,16,1536]{2,1,0:T(8,128)(2,1)S(1)}, bf16[16,16,1536]{2,1,0:T(8,128)(2,1)S(1)}, u32[]{:S(2)}, u32[]{:S(2)}) collective-permute-start(bf16[16,16,1536]{2,1,0:T(8,128)(2,1)S(1)} %all-to-all-done.mine), channel_id=1, source_target_pairs={{1,0},{0,1},{3,2},{2,3},{5,4},{4,5},{7,6},{6,7},{9,8},{8,9},{11,10... | collective-permute-start | bytes 2359304 | tf_op jit(solution)/shard_map/ppermute | solution.py:36
  55.9 4.2 %collective-permute-start.5 = (bf16[16,16,1536]{2,1,0:T(8,128)(2,1)S(1)}, bf16[16,16,1536]{2,1,0:T(8,128)(2,1)S(1)}, u32[]{:S(2)}, u32[]{:S(2)}) collective-permute-start(bf16[16,16,1536]{2,1,0:T(8,128)(2,1)S(1)} %collective-permute-done.2.ahead), channel_id=1, source_target_pairs={{1,0},{0,1},{3,2},{2,3},{5,4},{4,5},{7,6},{6,7},{9,8},{8,9},{11,10... | collective-permute-start | bytes 2359304 | tf_op jit(solution)/shard_map/ppermute | solution.py:36
  64.4 12.8 %collective-permute-start.7 = (bf16[3,3,6,512]{3,2,1,0:T(8,128)(2,1)S(1)}, bf16[3,3,6,512]{3,2,1,0:T(8,128)(2,1)S(1)}, u32[]{:S(2)}, u32[]{:S(2)}) collective-permute-start(bf16[3,3,6,512]{3,2,1,0:T(8,128)(2,1)S(1)} %reshape.22), channel_id=1, source_target_pairs={{0,32},{1,481},{2,34},{3,483},{4,36},{5,485},{6,38},{7,487},{8,40}... | collective-permute-start | bytes 165896 | tf_op jit(solution)/shard_map/ppermute | solution.py:41
  68.3 9.9 %collective-permute-start.8 = (bf16[3,3,6,512]{3,2,1,0:T(8,128)(2,1)S(1)}, bf16[3,3,6,512]{3,2,1,0:T(8,128)(2,1)S(1)}, u32[]{:S(2)}, u32[]{:S(2)}) collective-permute-start(bf16[3,3,6,512]{3,2,1,0:T(8,128)(2,1)S(1)} %reshape.23), channel_id=1, source_target_pairs={{0,33},{1,482},{2,35},{3,484},{4,37},{5,486},{6,39},{7,488},{8,41}... | collective-permute-start | bytes 165896 | tf_op jit(solution)/shard_map/ppermute | solution.py:41
  75.3 3.3 %collective-permute-start.6 = (bf16[3,3,6,512]{3,2,1,0:T(8,128)(2,1)S(1)}, bf16[3,3,6,512]{3,2,1,0:T(8,128)(2,1)S(1)}, u32[]{:S(2)}, u32[]{:S(2)}) collective-permute-start(bf16[3,3,6,512]{3,2,1,0:T(8,128)(2,1)S(1)} %reshape.21), channel_id=1, source_target_pairs={{0,1},{1,2},{2,3},{3,4},{4,5},{5,6},{6,7},{7,8},{8,9},{9,10},{10,1... | collective-permute-start | bytes 165896 | tf_op jit(solution)/shard_map/ppermute | solution.py:41

commit v5 on v4

--- a/solution.py
+++ b/solution.py
@@ -132,7 +132,10 @@
     labels,
     base,
     gain,
-    out,
+    own,
+    east,
+    band,
+    corner,
     weights,
     values,
 ):
@@ -215,8 +218,11 @@
         attended.append((sums / total).astype(bf16))
     attended = jnp.concatenate(attended, axis=1)
     result = jnp.dot(attended, weight(5 * width, 6 * width), preferred_element_type=f32)
-    result = (full + result.astype(bf16).astype(f32)).astype(bf16)
-    out[...] = result.reshape(latents, cells, width)
+    result = full + result.astype(bf16).astype(f32)
+    for k, out in enumerate((own, east, band, corner)):
+        for m in range(latents):
+            at = m * cells + k * CELLS
+            out[m] = result[at : at + CELLS].astype(bf16)
 
 
 def body(
@@ -294,9 +300,9 @@
     ahead_swapped = fetch(ahead, other_core)
     out = pl.pallas_call(
         functools.partial(window_kernel, HEADS, pool_heads),
-        out_shape=jax.ShapeDtypeStruct((latents, PADDED, width), jnp.bfloat16),
+        out_shape=[jax.ShapeDtypeStruct((latents, CELLS, width), jnp.bfloat16)] * 4,
         in_specs=[smem] + [vmem] * 9,
-        out_specs=vmem,
+        out_specs=[vmem] * 4,
         scratch_shapes=[
             pltpu.VMEM((groups, 2, piece_rows, all_columns), jnp.bfloat16),
             pltpu.VMEM((token_rows, width), jnp.float32),
@@ -317,7 +323,7 @@
     )
 
     def part_of(k):
-        return out[:, k * CELLS : (k + 1) * CELLS].reshape(latents, HALF_LAT, HALF_LON, width)
+        return out[k].reshape(latents, HALF_LAT, HALF_LON, width)
 
     to_band = give_back(part_of(2), along)
     to_corner = give_back(part_of(3), across)

time: 79.9 us -> 78.2 us (0.979)
  the two profiles are of different devices: /device:TPU:1 before, /device:TPU:6 now
where the time goes in v5:
time: 78.2 us; the launch traced here: 77.7 us
  starting transfers between devices  52.1 us (67%)
  waiting for transfers between devices  16.1 us (21%)
  Pallas kernels  6.46 us (8%)
  other arithmetic  1.72 us (2%)
  local copies, waits for them, and re-layouts  1.11 us (1%)
    ppermute x6, starting transfers between devices, fetch(): return lax.ppermute(block, BOTH, route)  29.6 us
    all_to_all x1, starting transfers between devices, body(): lax.all_to_all(mine, 'lon', 0, 0, tiled=True, axis_index_groups=same_core)  11.6 us
    ppermute x3, starting transfers between devices, give_back(): return lax.ppermute(block, BOTH, [(b, a) for a, b in route])  11 us
    ppermute x6, waiting for transfers between devices, fetch(): return lax.ppermute(block, BOTH, route)  7.26 us
    ppermute x3, waiting for transfers between devices, give_back(): return lax.ppermute(block, BOTH, [(b, a) for a, b in route])  5.81 us
    pallas_call x1, Pallas kernels, body(): pl.pallas_call(functools.partial(window_kernel, HEADS, pool_heads), out_s...  4.11 us
    all_to_all x1, waiting for transfers between devices, body(): lax.all_to_all(mine, 'lon', 0, 0, tiled=True, axis_index_groups=same_core)  3.03 us
  transfers between devices with their start and end apart: 10, of which 6 were waited for; matrix products, arithmetic and copies ran while one was open for 0% of the time, Pallas kernels for 3%

profile of v5, /device:TPU:6, one launch (start us, length us, event | category | flops | bytes accessed | tf_op | source)
XLA Modules:
  0.0 77.7 jit_solution(16621898442591166737)
XLA Ops:
  0.0 0.8 %fusion.2 = bf16[16,1536]{1,0:T(8,128)(2,1)S(1)} fusion(s32[]{:T(128)S(6)} %select_n.39, bf16[16,512]{1,0:T(8,128)(2,1)} %param.11, bf16[16,512]{1,0:T(8,128)(2,1)} %param.12, bf16[16,1536]{1,0:T(8,128)(2,1)} %param.15, bf16[16,512]{1,0:T(8,128)(2,1)} %param.16), kind=kLoop, calls=%fused_computation.7 | loop fusion | flops 196608 | bytes 147460 | tf_op jit(solution)/shard_map/concatenate | solution.py:246
  0.8 0.0 copy-start
  0.8 0.0 copy-start.2
  0.8 1.0 %broadcast_in_dim.2 = bf16[16,16,1536]{2,1,0:T(8,128)(2,1)} broadcast(bf16[16,1536]{1,0:T(8,128)(2,1)S(1)} %fusion.2), dimensions={1,2} | broadcast | bytes 835584 | tf_op jit(solution)/shard_map/broadcast_in_dim | solution.py:251
  1.8 0.0 copy-start.1
  1.8 11.6 %all-to-all-start = ((bf16[16,16,1536]{2,1,0:T(8,128)(2,1)}), bf16[16,16,1536]{2,1,0:T(8,128)(2,1)S(1)}, u32[]{:S(2)}, u32[]{:S(2)}) async-start(bf16[16,16,1536]{2,1,0:T(8,128)(2,1)} %broadcast_in_dim.2), calls=%async_computation | async-start | bytes 1572864 | tf_op jit(solution)/shard_map/all_to_all | solution.py:253
  13.4 0.0 copy-start.3
  13.4 0.0 copy-start.4
  13.4 0.1 pad_add_fusion.place
  13.5 0.0 copy-done
  13.5 0.0 copy-done.2
  13.5 0.9 %quarters.1 = (bf16[240,512]{1,0:T(8,128)(2,1)S(1)}, bf16[240,512]{1,0:T(8,128)(2,1)S(1)}, bf16[240,512]{1,0:T(8,128)(2,1)S(1)}, bf16[240,512]{1,0:T(8,128)(2,1)S(1)}) custom-call(s32[3]{0:T(128)S(1)} %pad_add_fusion.place, s32[6,12]{1,0:T(8,128)S(1)} %copy-done.2, bf16[6,12,13,512]{3,2,1,0:T(8,128)(2,1)S(1)} %bitcast.6), custom_call_target="tpu_custom_call" | custom-call | tf_op jit(solution)/shard_map/quarters/pallas_call | solution.py:261
  14.4 5.5 %collective-permute-start = (bf16[240,512]{1,0:T(8,128)(2,1)S(1)}, bf16[240,512]{1,0:T(8,128)(2,1)S(1)}, u32[]{:S(2)}, u32[]{:S(2)}) collective-permute-start(bf16[240,512]{1,0:T(8,128)(2,1)S(1)} %get-tuple-element.23), channel_id=1, source_target_pairs={{32,0},{481,1},{34,2},{483,3},{36,4},{485,5},{38,6},{487,7},{40,8}... | collective-permute-start | bytes 737288 | tf_op jit(solution)/shard_map/ppermute | solution.py:36
  19.9 5.9 %collective-permute-start.1 = (bf16[240,512]{1,0:T(8,128)(2,1)S(1)}, bf16[240,512]{1,0:T(8,128)(2,1)S(1)}, u32[]{:S(2)}, u32[]{:S(2)}) collective-permute-start(bf16[240,512]{1,0:T(8,128)(2,1)S(1)} %get-tuple-element.24), channel_id=1, source_target_pairs={{33,0},{482,1},{35,2},{484,3},{37,4},{486,5},{39,6},{488,7},{41,8}... | collective-permute-start | bytes 737288 | tf_op jit(solution)/shard_map/ppermute | solution.py:36
  25.8 0.0 collective-permute-done.band
  25.8 5.1 %collective-permute-done.1.corner = bf16[240,512]{1,0:T(8,128)(2,1)S(1)} collective-permute-done((bf16[240,512]{1,0:T(8,128)(2,1)S(1)}, bf16[240,512]{1,0:T(8,128)(2,1)S(1)}, u32[]{:S(2)}, u32[]{:S(2)}) %collective-permute-start.1) | collective-permute-done | bytes 245792 | tf_op jit(solution)/shard_map/ppermute | solution.py:36
  30.9 3.0 %all-to-all-done.mine = bf16[16,16,1536]{2,1,0:T(8,128)(2,1)S(1)} async-done(((bf16[16,16,1536]{2,1,0:T(8,128)(2,1)}), bf16[16,16,1536]{2,1,0:T(8,128)(2,1)S(1)}, u32[]{:S(2)}, u32[]{:S(2)}) %all-to-all-start) | async-done | bytes 786464 | tf_op jit(solution)/shard_map/all_to_all | solution.py:253
  33.9 2.8 %collective-permute-start.2 = (bf16[16,16,1536]{2,1,0:T(8,128)(2,1)S(1)}, bf16[16,16,1536]{2,1,0:T(8,128)(2,1)S(1)}, u32[]{:S(2)}, u32[]{:S(2)}) collective-permute-start(bf16[16,16,1536]{2,1,0:T(8,128)(2,1)S(1)} %all-to-all-done.mine), channel_id=1, source_target_pairs={{128,0},{385,1},{130,2},{387,3},{132,4},{389,5},{134,6},{391,7},{1... | collective-permute-start | bytes 2359304 | tf_op jit(solution)/shard_map/ppermute | solution.py:36
  36.7 8.7 %collective-permute-start.3 = (bf16[240,512]{1,0:T(8,128)(2,1)S(1)}, bf16[240,512]{1,0:T(8,128)(2,1)S(1)}, u32[]{:S(2)}, u32[]{:S(2)}) collective-permute-start(bf16[240,512]{1,0:T(8,128)(2,1)S(1)} %get-tuple-element.27), channel_id=1, source_target_pairs={{1,0},{2,1},{3,2},{4,3},{5,4},{6,5},{7,6},{8,7},{9,8},{10,9},{11,1... | collective-permute-start | bytes 737288 | tf_op jit(solution)/shard_map/ppermute | solution.py:36
  45.5 1.9 %collective-permute-start.4 = (bf16[16,16,1536]{2,1,0:T(8,128)(2,1)S(1)}, bf16[16,16,1536]{2,1,0:T(8,128)(2,1)S(1)}, u32[]{:S(2)}, u32[]{:S(2)}) collective-permute-start(bf16[16,16,1536]{2,1,0:T(8,128)(2,1)S(1)} %all-to-all-done.mine), channel_id=1, source_target_pairs={{1,0},{0,1},{3,2},{2,3},{5,4},{4,5},{7,6},{6,7},{9,8},{8,9},{11,10... | collective-permute-start | bytes 2359304 | tf_op jit(solution)/shard_map/ppermute | solution.py:36
  47.4 1.8 %collective-permute-done.3.east = bf16[240,512]{1,0:T(8,128)(2,1)S(1)} collective-permute-done((bf16[240,512]{1,0:T(8,128)(2,1)S(1)}, bf16[240,512]{1,0:T(8,128)(2,1)S(1)}, u32[]{:S(2)}, u32[]{:S(2)}) %collective-permute-start.3) | collective-permute-done | bytes 245792 | tf_op jit(solution)/shard_map/ppermute | solution.py:36
  49.2 0.0 collective-permute-done.2.ahead
  49.2 4.8 %collective-permute-start.5 = (bf16[16,16,1536]{2,1,0:T(8,128)(2,1)S(1)}, bf16[16,16,1536]{2,1,0:T(8,128)(2,1)S(1)}, u32[]{:S(2)}, u32[]{:S(2)}) collective-permute-start(bf16[16,16,1536]{2,1,0:T(8,128)(2,1)S(1)} %collective-permute-done.2.ahead), channel_id=1, source_target_pairs={{1,0},{0,1},{3,2},{2,3},{5,4},{4,5},{7,6},{6,7},{9,8},{8,9},{11,10... | collective-permute-start | bytes 2359304 | tf_op jit(solution)/shard_map/ppermute | solution.py:36
  53.9 0.0 copy-done.1
  53.9 1.5 %mix.1 = (bf16[1040,512]{1,0:T(8,128)(2,1)S(1)}, bf16[1040,48]{1,0:T(8,128)(2,1)S(1)}, f32[8,128]{1,0:T(8,128)S(1)}) custom-call(s32[3]{0:T(128)S(1)} %pad_add_fusion.place, bf16[240,512]{1,0:T(8,128)(2,1)S(1)} %get-tuple-element.22.own, bf16[240,512]{1,0:T(8,128)(2,1)S(1)} %collective-permute-done.3.east, bf16[240,512]{1,0:T(8,128)(2,1)S(1)} %collective-permute-done.band, ...), custom_call_target="tpu_custom_call" | custom-call | flops 51118080 | bytes 8388608 | tf_op jit(solution)/shard_map/mix/pallas_call | solution.py:280
  55.4 0.0 collective-permute-done.4.mine_swapped
  55.4 0.4 collective-permute-done.5.ahead_swapped
  55.8 0.0 copy-done.3
  55.8 0.0 copy-done.4
  55.8 4.1 %window.1 = (bf16[3,18,512]{2,1,0:T(8,128)(2,1)S(1)}, bf16[3,18,512]{2,1,0:T(8,128)(2,1)S(1)}, bf16[3,18,512]{2,1,0:T(8,128)(2,1)S(1)}, bf16[3,18,512]{2,1,0:T(8,128)(2,1)S(1)}) custom-call(s32[3]{0:T(128)S(1)} %pad_add_fusion.place, bf16[1040,512]{1,0:T(8,128)(2,1)S(1)} %get-tuple-element.31.tokens, bf16[1040,48]{1,0:T(8,128)(2,1)S(1)} %get-tuple-element.32.mix, ...), custom_call_target="tpu_custom_call" | custom-call | tf_op jit(solution)/shard_map/window/pallas_call | solution.py:301
  60.0 4.6 %collective-permute-start.8 = (bf16[3,3,6,512]{3,2,1,0:T(8,128)(2,1)S(1)}, bf16[3,3,6,512]{3,2,1,0:T(8,128)(2,1)S(1)}, u32[]{:S(2)}, u32[]{:S(2)}) collective-permute-start(bf16[3,3,6,512]{3,2,1,0:T(8,128)(2,1)S(1)} %reshape.23), channel_id=1, source_target_pairs={{0,33},{1,482},{2,35},{3,484},{4,37},{5,486},{6,39},{7,488},{8,41}... | collective-permute-start | bytes 165896 | tf_op jit(solution)/shard_map/ppermute | solution.py:41
  64.7 4.5 %collective-permute-start.7 = (bf16[3,3,6,512]{3,2,1,0:T(8,128)(2,1)S(1)}, bf16[3,3,6,512]{3,2,1,0:T(8,128)(2,1)S(1)}, u32[]{:S(2)}, u32[]{:S(2)}) collective-permute-start(bf16[3,3,6,512]{3,2,1,0:T(8,128)(2,1)S(1)} %reshape.22), channel_id=1, source_target_pairs={{0,32},{1,481},{2,34},{3,483},{4,36},{5,485},{6,38},{7,487},{8,40}... | collective-permute-start | bytes 165896 | tf_op jit(solution)/shard_map/ppermute | solution.py:41
  69.1 1.9 %collective-permute-start.6 = (bf16[3,3,6,512]{3,2,1,0:T(8,128)(2,1)S(1)}, bf16[3,3,6,512]{3,2,1,0:T(8,128)(2,1)S(1)}, u32[]{:S(2)}, u32[]{:S(2)}) collective-permute-start(bf16[3,3,6,512]{3,2,1,0:T(8,128)(2,1)S(1)} %reshape.21), channel_id=1, source_target_pairs={{0,1},{1,2},{2,3},{3,4},{4,5},{5,6},{6,7},{7,8},{8,9},{9,10},{10,1... | collective-permute-start | bytes 165896 | tf_op jit(solution)/shard_map/ppermute | solution.py:41
  71.1 0.0 collective-permute-done.8
  71.1 2.8 %collective-permute-done.7 = bf16[3,3,6,512]{3,2,1,0:T(8,128)(2,1)S(1)} collective-permute-done((bf16[3,3,6,512]{3,2,1,0:T(8,128)(2,1)S(1)}, bf16[3,3,6,512]{3,2,1,0:T(8,128)(2,1)S(1)}, u32[]{:S(2)}, u32[]{:S(2)}) %collective-permute-start.7) | collective-permute-done | bytes 55328 | tf_op jit(solution)/shard_map/ppermute | solution.py:41
  73.9 3.0 %collective-permute-done.6 = bf16[3,3,6,512]{3,2,1,0:T(8,128)(2,1)S(1)} collective-permute-done((bf16[3,3,6,512]{3,2,1,0:T(8,128)(2,1)S(1)}, bf16[3,3,6,512]{3,2,1,0:T(8,128)(2,1)S(1)}, u32[]{:S(2)}, u32[]{:S(2)}) %collective-permute-start.6) | collective-permute-done | bytes 55328 | tf_op jit(solution)/shard_map/ppermute | solution.py:41
  76.9 0.8 %maximum_select_fusion = bf16[3,6,12,512]{3,2,1,0:T(8,128)(2,1)} fusion(bf16[3,3,6,512]{3,2,1,0:T(8,128)(2,1)S(1)} %reshape.24, bf16[3,3,6,512]{3,2,1,0:T(8,128)(2,1)S(1)} %collective-permute-done.8, bf16[3,3,6,512]{3,2,1,0:T(8,128)(2,1)S(1)} %collective-permute-done.7, bf16[3,3,6,512]{3,2,1,0:T(8,128)(2,1)S(1)} %collective-permute-done.6, pred[]{:T(512)S(6)} %eq.11), kind=kLoop, calls=%fused_computation | loop fusion | flops 1880064 | bytes 442369 | tf_op jit(solution)/shard_map/jit(_where)/select_n | solution.py:333
  (4 shorter events, 0.1 us)
Async XLA Ops:
  0.8 12.7 %copy-start = (bf16[13,6,12,512]{3,0,2,1:T(8,128)(2,1)S(1)}, bf16[13,6,12,512]{3,0,2,1:T(8,128)(2,1)}, u32[]{:S(2)}) copy-start(bf16[13,6,12,512]{3,0,2,1:T(8,128)(2,1)} %param.9) | copy-start | bytes 2875396
  0.8 12.7 %copy-start.2 = (s32[6,12]{1,0:T(8,128)S(1)}, s32[6,12]{1,0:T(8,128)}, u32[]{:S(2)}) copy-start(s32[6,12]{1,0:T(8,128)} %regions.1) | copy-start | bytes 868
  1.8 52.1 %copy-start.1 = (bf16[3,16,512]{2,1,0:T(8,128)(2,1)S(1)}, bf16[3,16,512]{2,1,0:T(8,128)(2,1)}, u32[]{:S(2)}) copy-start(bf16[3,16,512]{2,1,0:T(8,128)(2,1)} %param.10) | copy-start | bytes 147460
  1.8 32.1 %all-to-all-start = ((bf16[16,16,1536]{2,1,0:T(8,128)(2,1)}), bf16[16,16,1536]{2,1,0:T(8,128)(2,1)S(1)}, u32[]{:S(2)}, u32[]{:S(2)}) async-start(bf16[16,16,1536]{2,1,0:T(8,128)(2,1)} %broadcast_in_dim.2), calls=%async_computation | async-start | bytes 1572864 | tf_op jit(solution)/shard_map/all_to_all | solution.py:253
  13.4 42.4 %copy-start.3 = (bf16[3,512]{1,0:T(4,128)(2,1)S(1)}, bf16[3,512]{1,0:T(4,128)(2,1)}, u32[]{:S(2)}) copy-start(bf16[3,512]{1,0:T(4,128)(2,1)} %base.1) | copy-start | bytes 9220
  13.4 42.4 %copy-start.4 = (f32[512]{0:T(512)S(1)}, f32[512]{0:T(512)}, u32[]{:S(2)}) copy-start(f32[512]{0:T(512)} %param.14) | copy-start | bytes 6148
  14.4 11.4 %collective-permute-start = (bf16[240,512]{1,0:T(8,128)(2,1)S(1)}, bf16[240,512]{1,0:T(8,128)(2,1)S(1)}, u32[]{:S(2)}, u32[]{:S(2)}) collective-permute-start(bf16[240,512]{1,0:T(8,128)(2,1)S(1)} %get-tuple-element.23), channel_id=1, source_target_pairs={{32,0},{481,1},{34,2},{483,3},{36,4},{485,5},{38,6},{487,7},{40,8}... | collective-permute-start | bytes 737288 | tf_op jit(solution)/shard_map/ppermute | solution.py:36
  19.9 11.0 %collective-permute-start.1 = (bf16[240,512]{1,0:T(8,128)(2,1)S(1)}, bf16[240,512]{1,0:T(8,128)(2,1)S(1)}, u32[]{:S(2)}, u32[]{:S(2)}) collective-permute-start(bf16[240,512]{1,0:T(8,128)(2,1)S(1)} %get-tuple-element.24), channel_id=1, source_target_pairs={{33,0},{482,1},{35,2},{484,3},{37,4},{486,5},{39,6},{488,7},{41,8}... | collective-permute-start | bytes 737288 | tf_op jit(solution)/shard_map/ppermute | solution.py:36
  33.9 15.2 %collective-permute-start.2 = (bf16[16,16,1536]{2,1,0:T(8,128)(2,1)S(1)}, bf16[16,16,1536]{2,1,0:T(8,128)(2,1)S(1)}, u32[]{:S(2)}, u32[]{:S(2)}) collective-permute-start(bf16[16,16,1536]{2,1,0:T(8,128)(2,1)S(1)} %all-to-all-done.mine), channel_id=1, source_target_pairs={{128,0},{385,1},{130,2},{387,3},{132,4},{389,5},{134,6},{391,7},{1... | collective-permute-start | bytes 2359304 | tf_op jit(solution)/shard_map/ppermute | solution.py:36
  36.7 12.4 %collective-permute-start.3 = (bf16[240,512]{1,0:T(8,128)(2,1)S(1)}, bf16[240,512]{1,0:T(8,128)(2,1)S(1)}, u32[]{:S(2)}, u32[]{:S(2)}) collective-permute-start(bf16[240,512]{1,0:T(8,128)(2,1)S(1)} %get-tuple-element.27), channel_id=1, source_target_pairs={{1,0},{2,1},{3,2},{4,3},{5,4},{6,5},{7,6},{8,7},{9,8},{10,9},{11,1... | collective-permute-start | bytes 737288 | tf_op jit(solution)/shard_map/ppermute | solution.py:36
  45.5 10.0 %collective-permute-start.4 = (bf16[16,16,1536]{2,1,0:T(8,128)(2,1)S(1)}, bf16[16,16,1536]{2,1,0:T(8,128)(2,1)S(1)}, u32[]{:S(2)}, u32[]{:S(2)}) collective-permute-start(bf16[16,16,1536]{2,1,0:T(8,128)(2,1)S(1)} %all-to-all-done.mine), channel_id=1, source_target_pairs={{1,0},{0,1},{3,2},{2,3},{5,4},{4,5},{7,6},{6,7},{9,8},{8,9},{11,10... | collective-permute-start | bytes 2359304 | tf_op jit(solution)/shard_map/ppermute | solution.py:36
  49.2 6.7 %collective-permute-start.5 = (bf16[16,16,1536]{2,1,0:T(8,128)(2,1)S(1)}, bf16[16,16,1536]{2,1,0:T(8,128)(2,1)S(1)}, u32[]{:S(2)}, u32[]{:S(2)}) collective-permute-start(bf16[16,16,1536]{2,1,0:T(8,128)(2,1)S(1)} %collective-permute-done.2.ahead), channel_id=1, source_target_pairs={{1,0},{0,1},{3,2},{2,3},{5,4},{4,5},{7,6},{6,7},{9,8},{8,9},{11,10... | collective-permute-start | bytes 2359304 | tf_op jit(solution)/shard_map/ppermute | solution.py:36
  60.0 11.0 %collective-permute-start.8 = (bf16[3,3,6,512]{3,2,1,0:T(8,128)(2,1)S(1)}, bf16[3,3,6,512]{3,2,1,0:T(8,128)(2,1)S(1)}, u32[]{:S(2)}, u32[]{:S(2)}) collective-permute-start(bf16[3,3,6,512]{3,2,1,0:T(8,128)(2,1)S(1)} %reshape.23), channel_id=1, source_target_pairs={{0,33},{1,482},{2,35},{3,484},{4,37},{5,486},{6,39},{7,488},{8,41}... | collective-permute-start | bytes 165896 | tf_op jit(solution)/shard_map/ppermute | solution.py:41
  64.7 9.3 %collective-permute-start.7 = (bf16[3,3,6,512]{3,2,1,0:T(8,128)(2,1)S(1)}, bf16[3,3,6,512]{3,2,1,0:T(8,128)(2,1)S(1)}, u32[]{:S(2)}, u32[]{:S(2)}) collective-permute-start(bf16[3,3,6,512]{3,2,1,0:T(8,128)(2,1)S(1)} %reshape.22), channel_id=1, source_target_pairs={{0,32},{1,481},{2,34},{3,483},{4,36},{5,485},{6,38},{7,487},{8,40}... | collective-permute-start | bytes 165896 | tf_op jit(solution)/shard_map/ppermute | solution.py:41
  69.1 7.8 %collective-permute-start.6 = (bf16[3,3,6,512]{3,2,1,0:T(8,128)(2,1)S(1)}, bf16[3,3,6,512]{3,2,1,0:T(8,128)(2,1)S(1)}, u32[]{:S(2)}, u32[]{:S(2)}) collective-permute-start(bf16[3,3,6,512]{3,2,1,0:T(8,128)(2,1)S(1)} %reshape.21), channel_id=1, source_target_pairs={{0,1},{1,2},{2,3},{3,4},{4,5},{5,6},{6,7},{7,8},{8,9},{9,10},{10,1... | collective-permute-start | bytes 165896 | tf_op jit(solution)/shard_map/ppermute | solution.py:41
